TPU v7x, 256 devices: a whole 4x4x8 slice. The times are simulated.
256 devices in a mesh: slab: 64 (over x, y_lo, z), fsdp: 4 (over y_hi, core).
Axes of the slice: x: 4, y: 4 (y_hi: 2, y_lo: 2; y = y_hi * 2 + y_lo), z: 8, core: 2. Of those that a mesh axis runs over, the one named last changes fastest.
Arguments:
- fields: bfloat16 [128, 128, 128, 128], P('slab', 'fsdp'), may hold values from -6 to 6
- cotangent: bfloat16 [128, 128, 128, 128], P('slab', 'fsdp'), may hold values from -6 to 6
- spectral: bfloat16 [16, 512, 2, 128, 128], P('fsdp', 'slab'), may hold values from -3 to 3
- pointwise: bfloat16 [128, 128], replicated, may hold values from -0.5 to 0.5
- lift_bias: float32 [128], replicated, may hold values from -3 to 3
Outputs:
- field_grads: bfloat16 [128, 128, 128, 128], P('slab', 'fsdp')
- weight_grads: float32 [16, 512, 2, 128, 128], P('fsdp', 'slab')
All inputs are finite; a program needn't handle non-finite values.
Results may differ from a plain program's by a relative error of at most 0.0043.
Values may be sent and summed in bfloat16 or wider, within the bound.
No kernel may reach another device: no remote copies, remote signals or barrier semaphores. Data moves between devices by JAX's collectives and lax.ppermute only.
A program may use at most 128 MiB of HBM per device.

v0:
```python
import math

import jax
import jax.numpy as jnp
import numpy as np
from jax import lax
from jax.experimental import pallas as pl
from jax.experimental.pallas import tpu as pltpu
from jax.sharding import PartitionSpec as P

MX = 16
MY = 16
MZ = 16
ROWS = 8
CORE_SWAP = [(0, 1), (1, 0), (2, 3), (3, 2)]
CHIP_SWAP = [(0, 2), (2, 0), (1, 3), (3, 1)]
VMEM_LIMIT = 24 * 1024 * 1024

f32 = jnp.float32
bf16 = jnp.bfloat16
highest = lax.Precision.HIGHEST


def waves(freqs, points, length):
    angle = 2.0 * math.pi / length * np.mod(np.outer(freqs, points), length)
    return np.cos(angle), np.sin(angle)


def complex_table(freqs, points, length):
    cosine, sine = waves(freqs, points, length)
    table = np.empty((len(freqs), 2, len(points), 2))
    table[:, 0, :, 0] = cosine
    table[:, 0, :, 1] = sine
    table[:, 1, :, 0] = -sine
    table[:, 1, :, 1] = cosine
    return table.astype(np.float32)


def real_table(freqs, points, length):
    cosine, sine = waves(freqs, points, length)
    return np.stack([cosine, -sine], 1).astype(np.float32)


def halves(table):
    table = np.asarray(table, np.float32)
    high = table.astype(bf16)
    low = (table - high.astype(np.float32)).astype(bf16)
    return jnp.asarray(high), jnp.asarray(low)


def high_low(table):
    table = np.asarray(table, np.float32)
    high = table.astype(bf16)
    return high, (table - high.astype(np.float32)).astype(bf16)


def z_tables(z_cells):
    wave = real_table(np.arange(MZ), np.arange(z_cells), z_cells).reshape(2 * MZ, z_cells)
    wave = np.einsum("kz,uv->ukvz", wave, np.eye(2, dtype=np.float32))
    high, low = high_low(wave.reshape(4 * MZ, 2 * z_cells))
    inverse = np.concatenate([high.T, low.T, high.T, low.T], axis=1)
    return jnp.asarray(np.concatenate([high, low, inverse], axis=0))


def y_tables(y_total, y_rows):
    freqs = np.concatenate([np.arange(MY), y_total - MY + np.arange(MY)])
    wave = complex_table(freqs, np.arange(y_total), y_total)
    wave = wave.reshape(2 * MY, 2, y_total // y_rows, y_rows, 2)
    table = np.einsum("jsfyr,qp->fjsqypr", wave, np.eye(4, dtype=np.float32))
    high, low = high_low(table.reshape(y_total // y_rows, 16 * MY, 8 * y_rows))
    turned = [np.swapaxes(part, 1, 2) for part in (high, low)]
    return jnp.asarray(np.concatenate([high, low] + turned, axis=1))


def product(form, left, right):
    return jnp.einsum(form, left, right, precision=highest)


def matmul(left, right):
    return jnp.dot(left, right, preferred_element_type=f32)


def matmul_t(left, right):
    return lax.dot_general(left, right, (((1,), (1,)), ((), ())), preferred_element_type=f32)


def split(value):
    high = value.astype(bf16)
    return high, (value - high.astype(f32)).astype(bf16)


def side(left, right):
    return jnp.concatenate([left, right], axis=1)


def gelu_slope(value):
    normal_cdf = 0.5 * (1.0 + lax.erf(value * (1.0 / math.sqrt(2.0))))
    return normal_cdf + value * jnp.exp(-0.5 * value * value) * (1.0 / math.sqrt(2.0 * math.pi))


def both_planes(ref, pair):
    start = 2 * pair
    shape = (2 * ref.shape[2], ref.shape[3])
    return side(ref[0, start:start + 2].reshape(shape), ref[1, start:start + 2].reshape(shape))


def put_planes(ref, pair, value):
    start = 2 * pair
    channels = ref.shape[3]
    shape = (2, ref.shape[2], channels)
    ref[0, start:start + 2] = value[:, :channels].reshape(shape)
    ref[1, start:start + 2] = value[:, channels:].reshape(shape)


def diagonal(square):
    zero = jnp.zeros_like(square)
    return jnp.concatenate([side(square, zero), side(zero, square)], axis=0)


def folded(table, value):
    result = matmul(table, value)
    count = result.shape[0] // 2
    return result[:count] + result[count:]


def first_row(half, owner):
    return pl.multiple_of(half * 16 + owner * 8, 8)


def y_forward(owner, lifted, y_table, target):
    channels = target.shape[-1]
    count = 16 * MY
    for half in range(2):
        block = lifted[:, pl.ds(first_row(half, owner), 8), :]
        high, low = split(block.reshape(block.shape[0] * 8, block.shape[2]))
        planes = folded(y_table[:2 * count], high) + matmul(y_table[:count], low)
        planes = planes.reshape(2 * MY, 8, 2 * channels)
        target[:, half, 0:8, :] = planes[:, :, :channels]
        target[:, half, 8:16, :] = planes[:, :, channels:]


def y_inverse(source, half, y_table):
    channels = source.shape[-1]
    planes = source[:, half].astype(f32)
    first = planes[:, 0:8, :].reshape(16 * MY, channels)
    second = planes[:, 8:16, :].reshape(16 * MY, channels)
    result = folded(y_table[32 * MY:], side(first, second).astype(bf16))
    return result.reshape(result.shape[0] // 8, 8, 2 * channels)


def keep_kernel(place, lifted, y_table, keep):
    y_forward(place[0], lifted, y_table, keep)


def keep_slopes_kernel(place, lifted, y_table, slopes, keep, slope_half, sems):
    copies = row_copies(slopes, slope_half, sems)
    for copy in copies:
        copy.start()
    y_forward(place[0], lifted, y_table, keep)
    for copy in copies:
        copy.wait()


def own_kernel(own, y_table, own_rows):
    for half in range(2):
        own_rows[half] = y_inverse(own, half, y_table)


def join_rows(core, own_rows, other, y_table, rows):
    for half in range(2):
        rows[:, pl.ds(first_row(half, core), 8), :] = own_rows[half]
        rows[:, pl.ds(first_row(half, 1 - core), 8), :] = y_inverse(other, half, y_table)


def z_inverse(pair, rows, z_table):
    value = rows[2 * pair:2 * pair + 2]
    high, low = split(value.reshape(4 * MZ, value.shape[2]))
    return matmul(z_table[8 * MZ:], jnp.concatenate([high, high, low, low], axis=0))


def put_lifted(lifted, pair, value):
    lifted[2 * pair:2 * pair + 2] = value.reshape(2, 2 * MZ, value.shape[1])


def row_copies(source, target, sems):
    copies = []
    count = source.shape[1] // sems.shape[0]
    for index in range(sems.shape[0]):
        span = slice(index * count, (index + 1) * count)
        copies.append(
            pltpu.make_async_copy(source.at[:, span], target.at[:, span], sems.at[index])
        )
    return copies


def put_rows(cells, target, sems, index):
    span = slice(index * ROWS, (index + 1) * ROWS)
    copy = pltpu.make_async_copy(cells.at[:, span], target.at[:, span], sems.at[index])
    copy.start()
    return copy


def lift_kernel(
    place, field, z_tables, y_tables, send, lifted, z_table, y_table, cells, sems, table_sems
):
    tables = [
        pltpu.make_async_copy(z_tables, z_table, table_sems.at[0]),
        pltpu.make_async_copy(y_tables.at[place[1]], y_table, table_sems.at[1]),
    ]
    copies = row_copies(field, cells, sems)
    for copy in (tables[0], *copies, tables[1]):
        copy.start()
    tables[0].wait()
    for pair in range(cells.shape[1] // 2):
        if pair % (ROWS // 2) == 0:
            copies[2 * pair // ROWS].wait()
        put_lifted(lifted, pair, folded(z_table[:8 * MZ], both_planes(cells, pair)))
    tables[1].wait()
    y_forward(1 - place[0], lifted, y_table, send)


def linear_rows(ref, pair, square, product_of):
    shape = (ROWS * ref.shape[2], ref.shape[3])
    span = slice(2 * pair, 2 * pair + ROWS)
    value = side(ref[0, span].reshape(shape), ref[1, span].reshape(shape))
    return product_of(value, square)


def slope_kernel(
    place, own_rows, other, field, cotangent, pointwise, bias, z_table, y_table,
    slope_half, send, lifted, rows,
):
    join_rows(place[0], own_rows, other, y_table, rows)
    square = diagonal(pointwise[...])
    shift = side(bias[...], bias[...])
    count = 2 * field.shape[2]
    for pair in range(field.shape[1] // 2):
        if pair % (ROWS // 2) == 0:
            linear = linear_rows(field, pair, square, matmul)
        start = pair % (ROWS // 2) * count
        pre = z_inverse(pair, rows, z_table) + linear[start:start + count] + shift
        slope = both_planes(cotangent, pair).astype(f32) * gelu_slope(pre)
        high, low = split(slope)
        put_planes(slope_half, pair, high)
        put_lifted(
            lifted, pair, folded(z_table[:8 * MZ], high) + matmul(z_table[:4 * MZ], low)
        )
    y_forward(1 - place[0], lifted, y_table, send)


def field_kernel(
    place, own_rows, other, slope_half, pointwise, z_table, y_table, result, rows, cells, sems
):
    copies = []
    join_rows(place[0], own_rows, other, y_table, rows)
    square = diagonal(pointwise[...])
    count = 2 * slope_half.shape[2]
    for pair in range(rows.shape[0] // 2):
        if pair % (ROWS // 2) == 0:
            linear = linear_rows(slope_half, pair, square, matmul_t)
        start = pair % (ROWS // 2) * count
        spatial = z_inverse(pair, rows, z_table)
        put_planes(cells, pair, (spatial + linear[start:start + count]).astype(bf16))
        if pair % (ROWS // 2) == ROWS // 2 - 1:
            copies.append(put_rows(cells, result, sems, 2 * pair // ROWS))
    for copy in copies:
        copy.wait()


def stage_kernel(source, target, sems):
    copies = row_copies(source, target, sems)
    for copy in copies:
        copy.start()
    for copy in copies:
        copy.wait()


def stacked_rows(values):
    parts = [split(value) for value in values]
    rows = [part[0].astype(f32) for part in parts] + [part[1].astype(f32) for part in parts]
    return jnp.concatenate(rows, axis=0)


def only(rows, pair):
    index = lax.broadcasted_iota(jnp.int32, rows.shape, 0)
    return jnp.where(index % 8 == pair, rows, 0.0).astype(bf16)


def side_weights(core, own, other, index, pair):
    block = other.at[index] if pair // 4 else own.at[index, core]
    return side(block[pair % 4, 0], block[pair % 4, 1])


def mix_kernel(place, modes, own, other, mixed):
    channels = modes.shape[-1]
    for index in range(modes.shape[0]):
        rows = stacked_rows([modes[index, 0], modes[index, 1]])
        total = jnp.zeros((32, 2 * channels), f32)
        for pair in range(8):
            weight = side_weights(place[0], own, other, index, pair)
            total = total + matmul(only(rows, pair), weight)
        real = total[0:8] + total[16:24]
        imag = total[8:16] + total[24:32]
        mixed[index, 0] = real[:, :channels] - imag[:, channels:]
        mixed[index, 1] = real[:, channels:] + imag[:, :channels]


def adjoint_kernel(place, grads, own, other, back):
    channels = grads.shape[-1]
    for index in range(grads.shape[0]):
        real, imag = grads[index, 0], grads[index, 1]
        rows = stacked_rows([side(real, imag), side(imag, -real)])
        total = jnp.zeros((32, channels), f32)
        for pair in range(8):
            weight = side_weights(place[0], own, other, index, pair)
            total = total + matmul_t(only(rows, pair), weight)
        back[index, 0] = total[0:8] + total[16:24]
        back[index, 1] = total[8:16] + total[24:32]


def outer_kernel(modes, grads, result):
    channels = modes.shape[-1]
    real, imag = grads[0, 0], grads[0, 1]
    left = stacked_rows([modes[0, 0], modes[0, 1]])
    right = stacked_rows([side(real, imag), side(imag, -real)])
    fill = channels - 48
    left = jnp.concatenate([left[:16], left[:16], left[16:], jnp.zeros((fill, channels), f32)], axis=0)
    right = jnp.concatenate([right, right[:16], jnp.zeros((fill, 2 * channels), f32)], axis=0)
    left = left.T
    right = right.astype(bf16)
    index = lax.broadcasted_iota(jnp.int32, left.shape, 1)
    for pair in range(8):
        value = matmul(jnp.where(index % 8 == pair, left, 0.0).astype(bf16), right)
        result[0, pair, 0] = value[:, :channels]
        result[0, pair, 1] = value[:, channels:]


def device_call(kernel, operands, spaces, outs, out_spaces, scratch, flops):
    operands = [
        pltpu.with_memory_space_constraint(operand, space) if space is pltpu.HBM else operand
        for operand, space in zip(operands, spaces)
    ]
    return pl.pallas_call(
        kernel,
        in_specs=[pl.BlockSpec(memory_space=space) for space in spaces],
        out_specs=[pl.BlockSpec(memory_space=space) for space in out_spaces],
        out_shape=outs,
        scratch_shapes=scratch,
        compiler_params=pltpu.CompilerParams(vmem_limit_bytes=VMEM_LIMIT),
        cost_estimate=pl.CostEstimate(flops=flops, bytes_accessed=10**6, transcendentals=0),
    )(*operands)


def modes_call(kernel, operands, out):
    def spec(array):
        rest = (0,) * (len(array.shape) - 1)
        return pl.BlockSpec((1,) + array.shape[1:], lambda step: (step,) + rest)

    return pl.pallas_call(
        kernel,
        grid=(out.shape[0],),
        in_specs=[spec(array) for array in operands],
        out_specs=spec(out),
        out_shape=out,
        compiler_params=pltpu.CompilerParams(vmem_limit_bytes=VMEM_LIMIT),
        cost_estimate=pl.CostEstimate(flops=10**9, bytes_accessed=4 * 10**6, transcendentals=0),
    )(*operands)


def own_first(pair, first):
    return jnp.where(first, pair[0], pair[1]), jnp.where(first, pair[1], pair[0])


def in_order(own, other, first):
    return jnp.where(first, own, other), jnp.where(first, other, own)


def body(fields, cotangent, spectral, pointwise, lift_bias):
    x_rows, y_rows, z_cells, channels = fields.shape
    slabs = lax.axis_size("slab")
    x_total = x_rows * slabs
    y_total = y_rows * lax.axis_size("fsdp")
    scale = 1.0 / float(x_total * y_total * z_cells)
    slab = lax.axis_index("slab")
    shard = lax.axis_index("fsdp")
    core_first = shard % 2 == 0
    chip_first = shard // 2 == 0
    place = jnp.stack([shard % 2, shard]).astype(jnp.int32)

    table_x = complex_table(np.arange(MX), np.arange(x_total), x_total)
    table_x = jnp.asarray(table_x.reshape(MX, 2, slabs, x_rows, 2))
    z_all = z_tables(z_cells)
    y_all = y_tables(y_total, y_rows)
    z_freq = (slab % 2) * 8 + (shard % 2) * 4 + jnp.arange(8, dtype=jnp.int32) % 4
    weight = jnp.where(z_freq == 0, scale, 2.0 * scale).astype(f32)
    own_weights = spectral.reshape(MX // 4, 2, 4, 2, channels, channels)
    send = lax.dynamic_index_in_dim(own_weights, 1 - shard % 2, 1, keepdims=False)
    other_weights = lax.ppermute(send, "fsdp", CORE_SWAP)

    message = jax.ShapeDtypeStruct((2 * MY, 2, 8 * x_rows, channels), f32)
    lifted_form = pltpu.VMEM((y_rows, 2 * MZ, 2 * channels), f32)
    own_form = pltpu.VMEM((2, y_rows, 8, 2 * channels), f32)

    def along(value):
        return value * weight[None, None, :, None]

    def to_modes(send, keep):
        planes = keep + lax.ppermute(send, "fsdp", CORE_SWAP)
        planes = planes.astype(bf16).reshape(slabs, x_rows * 8, channels)
        whole_x = lax.all_to_all(planes, "slab", split_axis=0, concat_axis=0, tiled=True)
        whole_x = whole_x.reshape(slabs, x_rows, 2, 4, channels).astype(f32)
        modes = product("xarqc,msxar->msqc", whole_x, table_x)
        keep, send = own_first(modes.reshape(2, MX // 2, 2, 4, channels), chip_first)
        modes = keep + lax.ppermute(send, "fsdp", CHIP_SWAP)
        return jnp.concatenate(own_first(modes.reshape(2, MX // 4, 2, 4, channels), core_first), 2)

    def regroup(modes):
        other = lax.ppermute(modes[..., 4:, :], "fsdp", CORE_SWAP)
        return jnp.concatenate(in_order(modes[..., :4, :], other, core_first), -2)

    def to_planes(modes, *beside):
        modes = jnp.concatenate(in_order(modes[:, :, :4], modes[:, :, 4:], core_first), 0)
        other = lax.ppermute(modes, "fsdp", CHIP_SWAP)
        modes = jnp.concatenate(in_order(modes, other, chip_first), 0)
        planes = product("msqc,msxar->xarqc", modes, table_x)
        planes = planes.astype(bf16).reshape(slabs, x_rows * 8, channels)
        planes = lax.all_to_all(planes, "slab", split_axis=0, concat_axis=0, tiled=True)
        planes, *beside = lax.optimization_barrier((planes, *beside))
        other = lax.ppermute(planes, "fsdp", CORE_SWAP)
        planes = planes.reshape(message.shape)
        own_rows, = device_call(
            own_kernel, (planes, y_table), (vmem, vmem), (own_form,), (vmem,), [], 10**9
        )
        return own_rows, other.reshape(message.shape), *beside

    smem, vmem, hbm = pltpu.SMEM, pltpu.VMEM, pltpu.HBM
    cells = pltpu.VMEM(fields.shape, bf16)
    sems = pltpu.SemaphoreType.DMA((y_rows // ROWS,))
    forms = (
        jax.ShapeDtypeStruct(z_all.shape, bf16), jax.ShapeDtypeStruct(y_all.shape[1:], bf16)
    )
    send, lifted, z_table, y_table = device_call(
        lift_kernel, (place, fields, z_all, y_all), (smem, hbm, hbm, hbm),
        (message, lifted_form) + forms, (vmem,) * 4,
        [cells, sems, pltpu.SemaphoreType.DMA((2,))], 10**9,
    )
    keep, = device_call(
        keep_kernel, (place, lifted, y_table), (smem, vmem, vmem), (message,), (vmem,), [], 10**9
    )
    modes = to_modes(send, keep)
    out = jax.ShapeDtypeStruct(modes.shape, f32)
    mixed, = device_call(
        mix_kernel, (place, modes, own_weights, other_weights), (smem,) + (vmem,) * 3,
        (out,), (vmem,), [], 10**9,
    )
    mixed = along(mixed)
    own_rows, other = to_planes(mixed)
    bias = lift_bias.reshape(1, channels)
    slopes, send, lifted = device_call(
        slope_kernel,
        (place, own_rows, other, fields, cotangent, pointwise, bias, z_table, y_table),
        (smem,) + (vmem,) * 8,
        (vmem(fields.shape, bf16), message, lifted_form), (vmem,) * 3,
        [lifted_form], 4 * 10**9,
    )
    keep, slope_half = device_call(
        keep_slopes_kernel, (place, lifted, y_table, slopes), (smem, vmem, vmem, vmem),
        (message, jax.ShapeDtypeStruct(fields.shape, bf16)), (vmem, hbm), [sems], 10**9,
    )
    grads = along(to_modes(send, keep))
    back, = device_call(
        adjoint_kernel, (place, grads, own_weights, other_weights), (smem,) + (vmem,) * 3,
        (out,), (vmem,), [], 10**9,
    )
    pair = regroup(jnp.stack([modes, grads]))
    weight_grads = modes_call(
        outer_kernel, (pair[0], pair[1]), jax.ShapeDtypeStruct(spectral.shape, f32)
    )
    back, slope_half = lax.optimization_barrier((back, slope_half))
    slopes, = device_call(
        stage_kernel, (slope_half,), (hbm,), (vmem(fields.shape, bf16),), (vmem,), [sems], 10**9
    )
    own_rows, other, weight_grads, slopes = to_planes(back, weight_grads, slopes)
    field_grads, = device_call(
        field_kernel, (place, own_rows, other, slopes, pointwise, z_table, y_table),
        (smem,) + (vmem,) * 6, (jax.ShapeDtypeStruct(fields.shape, bf16),), (hbm,),
        [lifted_form, cells, sems], 2 * 10**9,
    )
    return (field_grads, weight_grads)


def solution(mesh):
    in_specs = (
        P("slab", "fsdp", None, None),
        P("slab", "fsdp", None, None),
        P("fsdp", "slab", None, None, None),
        P(),
        P(),
    )
    out_specs = (P("slab", "fsdp", None, None), P("fsdp", "slab", None, None, None))
    return jax.shard_map(body, mesh=mesh, in_specs=in_specs, out_specs=out_specs, check_vma=False)
```

profile of v0, /device:TPU:1, one launch (start us, length us, event | category | flops | bytes accessed | tf_op | source)
XLA Modules:
  0.0 128.5 jit_solution(11382960407815692318)
XLA Ops:
  0.7 3.2 %shard_map.95 = (f32[32,2,16,128]{3,2,1,0:T(8,128)S(1)}, f32[32,32,256]{2,1,0:T(8,128)S(1)}, bf16[384,256]{1,0:T(8,128)(2,1)S(1)}, bf16[1024,256]{1,0:T(8,128)(2,1)S(1)}) custom-call(s32[2]{0:T(128)S(1)} %pad_add_fusion.place, bf16[2,32,128,128]{3,2,1,0:T(8,128)(2,1)} %field.3, bf16[384,256]{1,0:T(8,128)(2,1)} %constant.79.clone.z_tables, ...), custom_call_target="tpu_custom_call" | custom-call | flops 1000000000 | bytes 1000000 | tf_op jit(solution)/shard_map/pallas_call | solution.py:343
  3.9 3.3 %collective-permute-start = (f32[32,2,16,128]{3,2,1,0:T(8,128)S(1)}, f32[32,2,16,128]{3,2,1,0:T(8,128)S(1)}, u32[]{:S(2)}, u32[]{:S(2)}) collective-permute-start(f32[32,2,16,128]{3,2,1,0:T(8,128)S(1)} %get-tuple-element.18), channel_id=1, source_target_pairs={{0,1},{1,0},{2,3},{3,2},{4,5},{5,4},{6,7},{7,6},{8,9},{9,8},{10,11... | collective-permute-start | bytes 1572872 | tf_op jit(solution)/shard_map/ppermute | solution.py:408
  9.6 10.9 %all-to-all-start = ((bf16[64,16,128]{2,1,0:T(8,128)(2,1)}), bf16[64,16,128]{2,1,0:T(8,128)(2,1)S(1)}, u32[]{:S(2)}, u32[]{:S(2)}) async-start(bf16[64,16,128]{2,1,0:T(8,128)(2,1)} %bitcast.5), calls=%async_computation | async-start | bytes 524288 | tf_op jit(solution)/shard_map/all_to_all | solution.py:410
  22.2 10.2 %all-to-all-done = bf16[64,16,128]{2,1,0:T(8,128)(2,1)S(1)} async-done(((bf16[64,16,128]{2,1,0:T(8,128)(2,1)}), bf16[64,16,128]{2,1,0:T(8,128)(2,1)S(1)}, u32[]{:S(2)}, u32[]{:S(2)}) %all-to-all-start) | async-done | bytes 262176 | tf_op jit(solution)/shard_map/all_to_all | solution.py:410
  32.7 2.7 %collective-permute-start.1 = (f32[8,2,4,128]{3,2,1,0:T(4,128)S(1)}, f32[8,2,4,128]{3,2,1,0:T(4,128)S(1)}, u32[]{:S(2)}, u32[]{:S(2)}) collective-permute-start(f32[8,2,4,128]{3,2,1,0:T(4,128)S(1)} %copy_select_fusion.1), channel_id=1, source_target_pairs={{0,2},{2,0},{1,3},{3,1},{4,6},{6,4},{5,7},{7,5},{8,10},{10,8},{9,1... | collective-permute-start | bytes 98312 | tf_op jit(solution)/shard_map/ppermute | solution.py:414
  35.5 1.6 %collective-permute-done.1 = f32[8,2,4,128]{3,2,1,0:T(4,128)S(1)} collective-permute-done((f32[8,2,4,128]{3,2,1,0:T(4,128)S(1)}, f32[8,2,4,128]{3,2,1,0:T(4,128)S(1)}, u32[]{:S(2)}, u32[]{:S(2)}) %collective-permute-start.1) | collective-permute-done | bytes 32800 | tf_op jit(solution)/shard_map/ppermute | solution.py:414
  38.2 2.7 %collective-permute-start.3 = (f32[8,2,4,128]{3,2,1,0:T(4,128)S(1)}, f32[8,2,4,128]{3,2,1,0:T(4,128)S(1)}, u32[]{:S(2)}, u32[]{:S(2)}) collective-permute-start(f32[8,2,4,128]{3,2,1,0:T(4,128)S(1)} %pad_maximum_fusion.3), channel_id=1, source_target_pairs={{0,2},{2,0},{1,3},{3,1},{4,6},{6,4},{5,7},{7,5},{8,10},{10,8},{9,1... | collective-permute-start | bytes 98312 | tf_op jit(solution)/shard_map/ppermute | solution.py:423
  40.9 1.6 %collective-permute-done.3 = f32[8,2,4,128]{3,2,1,0:T(4,128)S(1)} collective-permute-done((f32[8,2,4,128]{3,2,1,0:T(4,128)S(1)}, f32[8,2,4,128]{3,2,1,0:T(4,128)S(1)}, u32[]{:S(2)}, u32[]{:S(2)}) %collective-permute-start.3) | collective-permute-done | bytes 32800 | tf_op jit(solution)/shard_map/ppermute | solution.py:423
  43.5 16.7 %all_to_all.20 = bf16[64,16,128]{2,1,0:T(8,128)(2,1)S(1)} all-to-all(bf16[64,16,128]{2,1,0:T(8,128)(2,1)S(1)} %copy.43), channel_id=1, replica_groups=mesh['slab'=64,'fsdp'=4] {'slab'}, dimensions={0} | all-to-all | bytes 524288 | tf_op jit(solution)/shard_map/all_to_all | solution.py:427
  60.2 5.0 %collective-permute-start.4 = (bf16[64,16,128]{2,1,0:T(8,128)(2,1)S(1)}, bf16[64,16,128]{2,1,0:T(8,128)(2,1)S(1)}, u32[]{:S(2)}, u32[]{:S(2)}) collective-permute-start(bf16[64,16,128]{2,1,0:T(8,128)(2,1)S(1)} %all_to_all.20), channel_id=1, source_target_pairs={{0,1},{1,0},{2,3},{3,2},{4,5},{5,4},{6,7},{7,6},{8,9},{9,8},{10,11... | collective-permute-start | bytes 786440 | tf_op jit(solution)/shard_map/ppermute | solution.py:429
  66.4 5.5 %shard_map.99 = (bf16[2,32,128,128]{3,2,1,0:T(8,128)(2,1)S(1)}, f32[32,2,16,128]{3,2,1,0:T(8,128)S(1)}, f32[32,32,256]{2,1,0:T(8,128)S(1)}) custom-call(s32[2]{0:T(128)S(1)} %pad_add_fusion.place, f32[2,32,8,256]{3,2,1,0:T(8,128)S(1)} %shard_map.98.own_rows, bf16[32,2,16,128]{3,2,1,0:T(8,128)(2,1)S(1)} %bitcast.74, bf16[2,32,128,128]{3,2,1,0:T(8,128)(2,1)S(1)} %copy-done, ...), custom_call_target="tpu_custom_call" | custom-call | flops 4000000000 | bytes 1000000 | tf_op jit(solution)/shard_map/pallas_call | solution.py:343
  72.6 1.1 shard_map.100
  74.2 16.0 %all_to_all.21 = bf16[64,16,128]{2,1,0:T(8,128)(2,1)S(1)} all-to-all(bf16[64,16,128]{2,1,0:T(8,128)(2,1)S(1)} %bitcast.77), channel_id=1, replica_groups=mesh['slab'=64,'fsdp'=4] {'slab'}, dimensions={0} | all-to-all | bytes 524288 | tf_op jit(solution)/shard_map/all_to_all | solution.py:410
  90.5 2.7 %collective-permute-start.6 = (f32[8,2,4,128]{3,2,1,0:T(4,128)S(1)}, f32[8,2,4,128]{3,2,1,0:T(4,128)S(1)}, u32[]{:S(2)}, u32[]{:S(2)}) collective-permute-start(f32[8,2,4,128]{3,2,1,0:T(4,128)S(1)} %copy_select_fusion), channel_id=1, source_target_pairs={{0,2},{2,0},{1,3},{3,1},{4,6},{6,4},{5,7},{7,5},{8,10},{10,8},{9,1... | collective-permute-start | bytes 98312 | tf_op jit(solution)/shard_map/ppermute | solution.py:414
  93.2 1.6 %collective-permute-done.6 = f32[8,2,4,128]{3,2,1,0:T(4,128)S(1)} collective-permute-done((f32[8,2,4,128]{3,2,1,0:T(4,128)S(1)}, f32[8,2,4,128]{3,2,1,0:T(4,128)S(1)}, u32[]{:S(2)}, u32[]{:S(2)}) %collective-permute-start.6) | collective-permute-done | bytes 32800 | tf_op jit(solution)/shard_map/ppermute | solution.py:414
  95.0 1.3 shard_map.101
  96.3 2.7 %collective-permute-start.7 = (f32[8,2,4,128]{3,2,1,0:T(4,128)S(1)}, f32[8,2,4,128]{3,2,1,0:T(4,128)S(1)}, u32[]{:S(2)}, u32[]{:S(2)}) collective-permute-start(f32[8,2,4,128]{3,2,1,0:T(4,128)S(1)} %pad_maximum_fusion.4), channel_id=1, source_target_pairs={{0,2},{2,0},{1,3},{3,1},{4,6},{6,4},{5,7},{7,5},{8,10},{10,8},{9,1... | collective-permute-start | bytes 98312 | tf_op jit(solution)/shard_map/ppermute | solution.py:423
  99.1 4.2 %collective-permute-start.8 = (f32[2,4,2,4,128]{4,3,2,1,0:T(4,128)S(1)}, f32[2,4,2,4,128]{4,3,2,1,0:T(4,128)S(1)}, u32[]{:S(2)}, u32[]{:S(2)}) collective-permute-start(f32[2,4,2,4,128]{4,3,2,1,0:T(4,128)S(1)} %pad_maximum_fusion.1), channel_id=1, source_target_pairs={{0,1},{1,0},{2,3},{3,2},{4,5},{5,4},{6,7},{7,6},{8,9},{9,8},{10,11... | collective-permute-start | bytes 98312 | tf_op jit(solution)/shard_map/ppermute | solution.py:418
  104.8 4.6 %all-to-all-start.3 = ((bf16[64,16,128]{2,1,0:T(8,128)(2,1)}), bf16[64,16,128]{2,1,0:T(8,128)(2,1)S(1)}, u32[]{:S(2)}, u32[]{:S(2)}) async-start(bf16[64,16,128]{2,1,0:T(8,128)(2,1)} %copy.51), calls=%async_computation.3 | async-start | bytes 524288 | tf_op jit(solution)/shard_map/all_to_all | solution.py:427
  109.4 1.6 %shard_map.103.slope_half = bf16[2,32,128,128]{3,2,1,0:T(8,128)(2,1)S(1)} custom-call(bf16[2,32,128,128]{3,2,1,0:T(8,128)(2,1)} %copy-done.1), custom_call_target="tpu_custom_call" | custom-call | flops 1000000000 | bytes 1000000 | tf_op jit(solution)/shard_map/pallas_call | solution.py:343
  111.1 3.0 %shard_map.102 = f32[4,8,2,128,128]{4,3,2,1,0:T(8,128)} custom-call(f32[4,2,8,128]{3,2,1,0:T(8,128)S(1)} %get-tuple-element.33.modes, f32[4,2,8,128]{3,2,1,0:T(8,128)S(1)} %get-tuple-element.32.grads), custom_call_target="tpu_custom_call" | custom-call | flops 1000000000 | bytes 4000000 | tf_op jit(solution)/shard_map/pallas_call | solution.py:359
  114.1 6.4 %all-to-all-done.3 = bf16[64,16,128]{2,1,0:T(8,128)(2,1)S(1)} async-done(((bf16[64,16,128]{2,1,0:T(8,128)(2,1)}), bf16[64,16,128]{2,1,0:T(8,128)(2,1)S(1)}, u32[]{:S(2)}, u32[]{:S(2)}) %all-to-all-start.3) | async-done | bytes 262176 | tf_op jit(solution)/shard_map/all_to_all | solution.py:427
  120.5 3.6 %collective-permute-start.9 = (bf16[64,16,128]{2,1,0:T(8,128)(2,1)S(1)}, bf16[64,16,128]{2,1,0:T(8,128)(2,1)S(1)}, u32[]{:S(2)}, u32[]{:S(2)}) collective-permute-start(bf16[64,16,128]{2,1,0:T(8,128)(2,1)S(1)} %all-to-all-done.3), channel_id=1, source_target_pairs={{0,1},{1,0},{2,3},{3,2},{4,5},{5,4},{6,7},{7,6},{8,9},{9,8},{10,11... | collective-permute-start | bytes 786440 | tf_op jit(solution)/shard_map/ppermute | solution.py:429
  125.3 3.0 %shard_map.105 = bf16[2,32,128,128]{3,2,1,0:T(8,128)(2,1)} custom-call(s32[2]{0:T(128)S(1)} %pad_add_fusion.place, f32[2,32,8,256]{3,2,1,0:T(8,128)S(1)} %shard_map.104.own_rows, bf16[32,2,16,128]{3,2,1,0:T(8,128)(2,1)S(1)} %bitcast.75, bf16[2,32,128,128]{3,2,1,0:T(8,128)(2,1)S(1)} %shard_map.103.slope_half, bf16[128,128]{1,0:T(8,128)(2,1)S(1)} %copy-done.10, ...), custom_call_target="tpu_custom_call" | custom-call | flops 2000000000 | bytes 1000000 | tf_op jit(solution)/shard_map/pallas_call | solution.py:343
  (77 shorter events, 12.0 us)
Async XLA Ops:
  3.9 5.7 %copy-start.4 = (bf16[1024,256]{1,0:T(8,128)(2,1)}, bf16[1024,256]{1,0:T(8,128)(2,1)S(1)}, u32[]{:S(2)}) copy-start(bf16[1024,256]{1,0:T(8,128)(2,1)S(1)} %get-tuple-element.17.y_table) | copy-start | bytes 1572868
  3.9 4.9 %collective-permute-start = (f32[32,2,16,128]{3,2,1,0:T(8,128)S(1)}, f32[32,2,16,128]{3,2,1,0:T(8,128)S(1)}, u32[]{:S(2)}, u32[]{:S(2)}) collective-permute-start(f32[32,2,16,128]{3,2,1,0:T(8,128)S(1)} %get-tuple-element.18), channel_id=1, source_target_pairs={{0,1},{1,0},{2,3},{3,2},{4,5},{5,4},{6,7},{7,6},{8,9},{9,8},{10,11... | collective-permute-start | bytes 1572872 | tf_op jit(solution)/shard_map/ppermute | solution.py:408
  7.2 13.3 %copy-start.2 = (bf16[4,8,2,128,128]{4,3,2,1,0:T(8,128)(2,1)S(1)}, bf16[4,8,2,128,128]{4,3,2,1,0:T(8,128)(2,1)}, u32[]{:S(2)}) copy-start(bf16[4,8,2,128,128]{4,3,2,1,0:T(8,128)(2,1)} %param.10) | copy-start | bytes 6291460
  8.2 24.2 %copy-start.13 = (f32[16,2,64,2,2,1]{2,0,4,3,5,1:T(8,128)S(1)}, f32[16,2,64,2,2,1]{2,0,4,3,5,1:T(8,128)}, u32[]{:S(2)}) copy-start(f32[16,2,64,2,2,1]{2,0,4,3,5,1:T(8,128)} %constant.84) | copy-start | bytes 98308
  9.6 22.8 %all-to-all-start = ((bf16[64,16,128]{2,1,0:T(8,128)(2,1)}), bf16[64,16,128]{2,1,0:T(8,128)(2,1)S(1)}, u32[]{:S(2)}, u32[]{:S(2)}) async-start(bf16[64,16,128]{2,1,0:T(8,128)(2,1)} %bitcast.5), calls=%async_computation | async-start | bytes 524288 | tf_op jit(solution)/shard_map/all_to_all | solution.py:410
  21.6 15.6 %collective-permute-start.2 = (bf16[4,4,2,128,128]{4,3,2,1,0:T(8,128)(2,1)}, bf16[4,4,2,128,128]{4,3,2,1,0:T(8,128)(2,1)S(1)}, u32[]{:S(2)}, u32[]{:S(2)}) collective-permute-start(bf16[4,4,2,128,128]{4,3,2,1,0:T(8,128)(2,1)} %dynamic-slice_bitcast_fusion), channel_id=1, source_target_pairs={{0,1},{1,0},{2,3},{3,2},{4,5},{5,4},{6,7},{7,6},{8,9},{9,8},{10,11... | collective-permute-start | bytes 3145736 | tf_op jit(solution)/shard_map/ppermute | solution.py:398
  32.7 4.4 %collective-permute-start.1 = (f32[8,2,4,128]{3,2,1,0:T(4,128)S(1)}, f32[8,2,4,128]{3,2,1,0:T(4,128)S(1)}, u32[]{:S(2)}, u32[]{:S(2)}) collective-permute-start(f32[8,2,4,128]{3,2,1,0:T(4,128)S(1)} %copy_select_fusion.1), channel_id=1, source_target_pairs={{0,2},{2,0},{1,3},{3,1},{4,6},{6,4},{5,7},{7,5},{8,10},{10,8},{9,1... | collective-permute-start | bytes 98312 | tf_op jit(solution)/shard_map/ppermute | solution.py:414
  38.1 27.1 %copy-start.5 = (bf16[1024,256]{1,0:T(8,128)(2,1)S(1)}, bf16[1024,256]{1,0:T(8,128)(2,1)}, u32[]{:S(2)}) copy-start(bf16[1024,256]{1,0:T(8,128)(2,1)} %copy-done.4) | copy-start | bytes 1572868
  38.2 4.4 %collective-permute-start.3 = (f32[8,2,4,128]{3,2,1,0:T(4,128)S(1)}, f32[8,2,4,128]{3,2,1,0:T(4,128)S(1)}, u32[]{:S(2)}, u32[]{:S(2)}) collective-permute-start(f32[8,2,4,128]{3,2,1,0:T(4,128)S(1)} %pad_maximum_fusion.3), channel_id=1, source_target_pairs={{0,2},{2,0},{1,3},{3,1},{4,6},{6,4},{5,7},{7,5},{8,10},{10,8},{9,1... | collective-permute-start | bytes 98312 | tf_op jit(solution)/shard_map/ppermute | solution.py:423
  43.3 23.1 %copy-start.8 = (bf16[384,256]{1,0:T(8,128)(2,1)S(1)}, bf16[384,256]{1,0:T(8,128)(2,1)}, u32[]{:S(2)}) copy-start(bf16[384,256]{1,0:T(8,128)(2,1)} %copy-done.7) | copy-start | bytes 589828
  43.5 22.9 %copy-start = (bf16[2,32,128,128]{3,2,1,0:T(8,128)(2,1)S(1)}, bf16[2,32,128,128]{3,2,1,0:T(8,128)(2,1)}, u32[]{:S(2)}) copy-start(bf16[2,32,128,128]{3,2,1,0:T(8,128)(2,1)} %field.3) | copy-start | bytes 6291460
  43.5 22.9 %copy-start.3 = (bf16[2,32,128,128]{3,2,1,0:T(8,128)(2,1)S(1)}, bf16[2,32,128,128]{3,2,1,0:T(8,128)(2,1)}, u32[]{:S(2)}) copy-start(bf16[2,32,128,128]{3,2,1,0:T(8,128)(2,1)} %cotangent.1) | copy-start | bytes 6291460
  43.5 22.9 %copy-start.10 = (bf16[128,128]{1,0:T(8,128)(2,1)S(1)}, bf16[128,128]{1,0:T(8,128)(2,1)}, u32[]{:S(2)}) copy-start(bf16[128,128]{1,0:T(8,128)(2,1)} %pointwise.3) | copy-start | bytes 98308
  43.5 22.9 %copy-start.11 = (f32[128]{0:T(128)S(1)}, f32[128]{0:T(128)}, u32[]{:S(2)}) copy-start(f32[128]{0:T(128)} %param.12) | copy-start | bytes 1540
  60.2 6.2 %collective-permute-start.4 = (bf16[64,16,128]{2,1,0:T(8,128)(2,1)S(1)}, bf16[64,16,128]{2,1,0:T(8,128)(2,1)S(1)}, u32[]{:S(2)}, u32[]{:S(2)}) collective-permute-start(bf16[64,16,128]{2,1,0:T(8,128)(2,1)S(1)} %all_to_all.20), channel_id=1, source_target_pairs={{0,1},{1,0},{2,3},{3,2},{4,5},{5,4},{6,7},{7,6},{8,9},{9,8},{10,11... | collective-permute-start | bytes 786440 | tf_op jit(solution)/shard_map/ppermute | solution.py:429
  71.9 2.2 %collective-permute-start.5 = (f32[32,2,16,128]{3,2,1,0:T(8,128)S(1)}, f32[32,2,16,128]{3,2,1,0:T(8,128)S(1)}, u32[]{:S(2)}, u32[]{:S(2)}) collective-permute-start(f32[32,2,16,128]{3,2,1,0:T(8,128)S(1)} %get-tuple-element.23), channel_id=1, source_target_pairs={{0,1},{1,0},{2,3},{3,2},{4,5},{5,4},{6,7},{7,6},{8,9},{9,8},{10,11... | collective-permute-start | bytes 1572872 | tf_op jit(solution)/shard_map/ppermute | solution.py:408
  73.7 22.5 %copy-start.1 = (bf16[2,32,128,128]{3,2,1,0:T(8,128)(2,1)}, bf16[2,32,128,128]{3,2,1,0:T(8,128)(2,1)S(1)}, u32[]{:S(2)}) copy-start(bf16[2,32,128,128]{3,2,1,0:T(8,128)(2,1)S(1)} %get-tuple-element.26.source) | copy-start | bytes 6291460
  90.5 4.4 %collective-permute-start.6 = (f32[8,2,4,128]{3,2,1,0:T(4,128)S(1)}, f32[8,2,4,128]{3,2,1,0:T(4,128)S(1)}, u32[]{:S(2)}, u32[]{:S(2)}) collective-permute-start(f32[8,2,4,128]{3,2,1,0:T(4,128)S(1)} %copy_select_fusion), channel_id=1, source_target_pairs={{0,2},{2,0},{1,3},{3,1},{4,6},{6,4},{5,7},{7,5},{8,10},{10,8},{9,1... | collective-permute-start | bytes 98312 | tf_op jit(solution)/shard_map/ppermute | solution.py:414
  96.3 7.0 %collective-permute-start.7 = (f32[8,2,4,128]{3,2,1,0:T(4,128)S(1)}, f32[8,2,4,128]{3,2,1,0:T(4,128)S(1)}, u32[]{:S(2)}, u32[]{:S(2)}) collective-permute-start(f32[8,2,4,128]{3,2,1,0:T(4,128)S(1)} %pad_maximum_fusion.4), channel_id=1, source_target_pairs={{0,2},{2,0},{1,3},{3,1},{4,6},{6,4},{5,7},{7,5},{8,10},{10,8},{9,1... | collective-permute-start | bytes 98312 | tf_op jit(solution)/shard_map/ppermute | solution.py:423
  99.1 11.9 %collective-permute-start.8 = (f32[2,4,2,4,128]{4,3,2,1,0:T(4,128)S(1)}, f32[2,4,2,4,128]{4,3,2,1,0:T(4,128)S(1)}, u32[]{:S(2)}, u32[]{:S(2)}) collective-permute-start(f32[2,4,2,4,128]{4,3,2,1,0:T(4,128)S(1)} %pad_maximum_fusion.1), channel_id=1, source_target_pairs={{0,1},{1,0},{2,3},{3,2},{4,5},{5,4},{6,7},{7,6},{8,9},{9,8},{10,11... | collective-permute-start | bytes 98312 | tf_op jit(solution)/shard_map/ppermute | solution.py:418
  104.8 15.6 %all-to-all-start.3 = ((bf16[64,16,128]{2,1,0:T(8,128)(2,1)}), bf16[64,16,128]{2,1,0:T(8,128)(2,1)S(1)}, u32[]{:S(2)}, u32[]{:S(2)}) async-start(bf16[64,16,128]{2,1,0:T(8,128)(2,1)} %copy.51), calls=%async_computation.3 | async-start | bytes 524288 | tf_op jit(solution)/shard_map/all_to_all | solution.py:427
  111.1 13.0 %copy-start.6 = (bf16[1024,256]{1,0:T(8,128)(2,1)S(1)}, bf16[1024,256]{1,0:T(8,128)(2,1)}, u32[]{:S(2)}) copy-start(bf16[1024,256]{1,0:T(8,128)(2,1)} %copy-done.4) | copy-start | bytes 1572868
  114.1 11.2 %copy-start.9 = (bf16[384,256]{1,0:T(8,128)(2,1)S(1)}, bf16[384,256]{1,0:T(8,128)(2,1)}, u32[]{:S(2)}) copy-start(bf16[384,256]{1,0:T(8,128)(2,1)} %copy-done.7) | copy-start | bytes 589828
  120.5 4.8 %collective-permute-start.9 = (bf16[64,16,128]{2,1,0:T(8,128)(2,1)S(1)}, bf16[64,16,128]{2,1,0:T(8,128)(2,1)S(1)}, u32[]{:S(2)}, u32[]{:S(2)}) collective-permute-start(bf16[64,16,128]{2,1,0:T(8,128)(2,1)S(1)} %all-to-all-done.3), channel_id=1, source_target_pairs={{0,1},{1,0},{2,3},{3,2},{4,5},{5,4},{6,7},{7,6},{8,9},{9,8},{10,11... | collective-permute-start | bytes 786440 | tf_op jit(solution)/shard_map/ppermute | solution.py:429
  (2 other events, 11.1 us)
where the time goes:
time: 129 us; the launch traced here: 128 us
  starting transfers between devices  43.8 us (34%)
  blocking collectives  32.7 us (25%)
  waiting for transfers between devices  24.2 us (19%)
  Pallas kernels  21.1 us (16%)
  local copies, waits for them, and re-layouts  2.25 us (2%)
  matrix products  1.78 us (1%)
  other arithmetic  1.46 us (1%)
    pallas_call x10, Pallas kernels, device_call(): pl.pallas_call(kernel, in_specs=[pl.BlockSpec(memory_space=space) for spa...  18.1 us
    all_to_all x1, blocking collectives, to_planes(): lax.all_to_all(planes, 'slab', split_axis=0, concat_axis=0, tiled=True)  16.7 us
    all_to_all x1, blocking collectives, to_modes(): lax.all_to_all(planes, 'slab', split_axis=0, concat_axis=0, tiled=True)  16 us
    all_to_all x1, starting transfers between devices, to_modes(): lax.all_to_all(planes, 'slab', split_axis=0, concat_axis=0, tiled=True)  10.9 us
    all_to_all x1, waiting for transfers between devices, to_modes(): lax.all_to_all(planes, 'slab', split_axis=0, concat_axis=0, tiled=True)  10.2 us
    ppermute x2, starting transfers between devices, to_planes(): other = lax.ppermute(planes, 'fsdp', CORE_SWAP)  8.67 us
    all_to_all x1, waiting for transfers between devices, to_planes(): lax.all_to_all(planes, 'slab', split_axis=0, concat_axis=0, tiled=True)  6.39 us
    ppermute x2, starting transfers between devices, to_planes(): other = lax.ppermute(modes, 'fsdp', CHIP_SWAP)  5.42 us
  transfers between devices with their start and end apart: 12, of which 9 were waited for; matrix products, arithmetic and copies ran while one was open for 2% of the time, Pallas kernels for 6%

commit v1 on v0

--- a/solution.py
+++ b/solution.py
@@ -18,7 +18,7 @@
 
 f32 = jnp.float32
 bf16 = jnp.bfloat16
-highest = lax.Precision.HIGHEST
+exact = lax.Precision.HIGH
 
 
 def waves(freqs, points, length):
@@ -73,7 +73,7 @@
 
 
 def product(form, left, right):
-    return jnp.einsum(form, left, right, precision=highest)
+    return jnp.einsum(form, left, right, precision=exact)
 
 
 def matmul(left, right):

time: 129 us -> 128 us (level)
  no operation moved by 1% of the time
where the time goes in v1:
time: 128 us
  starting transfers between devices  43.7 us (34%)
  blocking collectives  32.8 us (26%)
  waiting for transfers between devices  24.2 us (19%)
  Pallas kernels  21.1 us (16%)
  local copies, waits for them, and re-layouts  2.25 us (2%)
  other arithmetic  1.46 us (1%)
  matrix products  1.29 us (1%)
    pallas_call x10, Pallas kernels, device_call(): pl.pallas_call(kernel, in_specs=[pl.BlockSpec(memory_space=space) for spa...  18.1 us
    all_to_all x1, blocking collectives, to_planes(): lax.all_to_all(planes, 'slab', split_axis=0, concat_axis=0, tiled=True)  16.7 us
    all_to_all x1, blocking collectives, to_modes(): lax.all_to_all(planes, 'slab', split_axis=0, concat_axis=0, tiled=True)  16.1 us
    all_to_all x1, starting transfers between devices, to_modes(): lax.all_to_all(planes, 'slab', split_axis=0, concat_axis=0, tiled=True)  10.9 us
    all_to_all x1, waiting for transfers between devices, to_modes(): lax.all_to_all(planes, 'slab', split_axis=0, concat_axis=0, tiled=True)  10.2 us
    ppermute x2, starting transfers between devices, to_planes(): other = lax.ppermute(planes, 'fsdp', CORE_SWAP)  8.67 us
    all_to_all x1, waiting for transfers between devices, to_planes(): lax.all_to_all(planes, 'slab', split_axis=0, concat_axis=0, tiled=True)  6.39 us
    ppermute x2, starting transfers between devices, to_modes(): modes = keep + lax.ppermute(send, 'fsdp', CHIP_SWAP)  5.42 us
  transfers between devices with their start and end apart: 12, of which 9 were waited for; matrix products, arithmetic and copies ran while one was open for 2% of the time, Pallas kernels for 6%

profile of v1, /device:TPU:1, one launch (start us, length us, event | category | flops | bytes accessed | tf_op | source)
XLA Modules:
  0.0 128.0 jit_solution(11710091668880061718)
XLA Ops:
  0.7 3.2 %shard_map.95 = (f32[32,2,16,128]{3,2,1,0:T(8,128)S(1)}, f32[32,32,256]{2,1,0:T(8,128)S(1)}, bf16[384,256]{1,0:T(8,128)(2,1)S(1)}, bf16[1024,256]{1,0:T(8,128)(2,1)S(1)}) custom-call(s32[2]{0:T(128)S(1)} %pad_add_fusion.place, bf16[2,32,128,128]{3,2,1,0:T(8,128)(2,1)} %field.3, bf16[384,256]{1,0:T(8,128)(2,1)} %constant.79.clone.z_tables, ...), custom_call_target="tpu_custom_call" | custom-call | flops 1000000000 | bytes 1000000 | tf_op jit(solution)/shard_map/pallas_call | solution.py:343
  3.9 3.3 %collective-permute-start = (f32[32,2,16,128]{3,2,1,0:T(8,128)S(1)}, f32[32,2,16,128]{3,2,1,0:T(8,128)S(1)}, u32[]{:S(2)}, u32[]{:S(2)}) collective-permute-start(f32[32,2,16,128]{3,2,1,0:T(8,128)S(1)} %get-tuple-element.18), channel_id=1, source_target_pairs={{0,1},{1,0},{2,3},{3,2},{4,5},{5,4},{6,7},{7,6},{8,9},{9,8},{10,11... | collective-permute-start | bytes 1572872 | tf_op jit(solution)/shard_map/ppermute | solution.py:408
  9.6 10.9 %all-to-all-start = ((bf16[64,16,128]{2,1,0:T(8,128)(2,1)}), bf16[64,16,128]{2,1,0:T(8,128)(2,1)S(1)}, u32[]{:S(2)}, u32[]{:S(2)}) async-start(bf16[64,16,128]{2,1,0:T(8,128)(2,1)} %bitcast.5), calls=%async_computation | async-start | bytes 524288 | tf_op jit(solution)/shard_map/all_to_all | solution.py:410
  22.2 10.2 %all-to-all-done = bf16[64,16,128]{2,1,0:T(8,128)(2,1)S(1)} async-done(((bf16[64,16,128]{2,1,0:T(8,128)(2,1)}), bf16[64,16,128]{2,1,0:T(8,128)(2,1)S(1)}, u32[]{:S(2)}, u32[]{:S(2)}) %all-to-all-start) | async-done | bytes 262176 | tf_op jit(solution)/shard_map/all_to_all | solution.py:410
  32.7 2.7 %collective-permute-start.1 = (f32[8,2,4,128]{3,2,1,0:T(4,128)S(1)}, f32[8,2,4,128]{3,2,1,0:T(4,128)S(1)}, u32[]{:S(2)}, u32[]{:S(2)}) collective-permute-start(f32[8,2,4,128]{3,2,1,0:T(4,128)S(1)} %copy_select_fusion.1), channel_id=1, source_target_pairs={{0,2},{2,0},{1,3},{3,1},{4,6},{6,4},{5,7},{7,5},{8,10},{10,8},{9,1... | collective-permute-start | bytes 98312 | tf_op jit(solution)/shard_map/ppermute | solution.py:414
  35.4 1.6 %collective-permute-done.1 = f32[8,2,4,128]{3,2,1,0:T(4,128)S(1)} collective-permute-done((f32[8,2,4,128]{3,2,1,0:T(4,128)S(1)}, f32[8,2,4,128]{3,2,1,0:T(4,128)S(1)}, u32[]{:S(2)}, u32[]{:S(2)}) %collective-permute-start.1) | collective-permute-done | bytes 32800 | tf_op jit(solution)/shard_map/ppermute | solution.py:414
  38.2 2.7 %collective-permute-start.3 = (f32[8,2,4,128]{3,2,1,0:T(4,128)S(1)}, f32[8,2,4,128]{3,2,1,0:T(4,128)S(1)}, u32[]{:S(2)}, u32[]{:S(2)}) collective-permute-start(f32[8,2,4,128]{3,2,1,0:T(4,128)S(1)} %pad_maximum_fusion.3), channel_id=1, source_target_pairs={{0,2},{2,0},{1,3},{3,1},{4,6},{6,4},{5,7},{7,5},{8,10},{10,8},{9,1... | collective-permute-start | bytes 98312 | tf_op jit(solution)/shard_map/ppermute | solution.py:423
  40.9 1.6 %collective-permute-done.3 = f32[8,2,4,128]{3,2,1,0:T(4,128)S(1)} collective-permute-done((f32[8,2,4,128]{3,2,1,0:T(4,128)S(1)}, f32[8,2,4,128]{3,2,1,0:T(4,128)S(1)}, u32[]{:S(2)}, u32[]{:S(2)}) %collective-permute-start.3) | collective-permute-done | bytes 32800 | tf_op jit(solution)/shard_map/ppermute | solution.py:423
  43.3 16.7 %all_to_all.20 = bf16[64,16,128]{2,1,0:T(8,128)(2,1)S(1)} all-to-all(bf16[64,16,128]{2,1,0:T(8,128)(2,1)S(1)} %copy.43), channel_id=1, replica_groups=mesh['slab'=64,'fsdp'=4] {'slab'}, dimensions={0} | all-to-all | bytes 524288 | tf_op jit(solution)/shard_map/all_to_all | solution.py:427
  60.0 5.0 %collective-permute-start.4 = (bf16[64,16,128]{2,1,0:T(8,128)(2,1)S(1)}, bf16[64,16,128]{2,1,0:T(8,128)(2,1)S(1)}, u32[]{:S(2)}, u32[]{:S(2)}) collective-permute-start(bf16[64,16,128]{2,1,0:T(8,128)(2,1)S(1)} %all_to_all.20), channel_id=1, source_target_pairs={{0,1},{1,0},{2,3},{3,2},{4,5},{5,4},{6,7},{7,6},{8,9},{9,8},{10,11... | collective-permute-start | bytes 786440 | tf_op jit(solution)/shard_map/ppermute | solution.py:429
  66.2 5.5 %shard_map.99 = (bf16[2,32,128,128]{3,2,1,0:T(8,128)(2,1)S(1)}, f32[32,2,16,128]{3,2,1,0:T(8,128)S(1)}, f32[32,32,256]{2,1,0:T(8,128)S(1)}) custom-call(s32[2]{0:T(128)S(1)} %pad_add_fusion.place, f32[2,32,8,256]{3,2,1,0:T(8,128)S(1)} %shard_map.98.own_rows, bf16[32,2,16,128]{3,2,1,0:T(8,128)(2,1)S(1)} %bitcast.74, bf16[2,32,128,128]{3,2,1,0:T(8,128)(2,1)S(1)} %copy-done, ...), custom_call_target="tpu_custom_call" | custom-call | flops 4000000000 | bytes 1000000 | tf_op jit(solution)/shard_map/pallas_call | solution.py:343
  72.2 1.1 shard_map.100
  73.8 16.1 %all_to_all.21 = bf16[64,16,128]{2,1,0:T(8,128)(2,1)S(1)} all-to-all(bf16[64,16,128]{2,1,0:T(8,128)(2,1)S(1)} %bitcast.77), channel_id=1, replica_groups=mesh['slab'=64,'fsdp'=4] {'slab'}, dimensions={0} | all-to-all | bytes 524288 | tf_op jit(solution)/shard_map/all_to_all | solution.py:410
  90.2 2.7 %collective-permute-start.6 = (f32[8,2,4,128]{3,2,1,0:T(4,128)S(1)}, f32[8,2,4,128]{3,2,1,0:T(4,128)S(1)}, u32[]{:S(2)}, u32[]{:S(2)}) collective-permute-start(f32[8,2,4,128]{3,2,1,0:T(4,128)S(1)} %copy_select_fusion), channel_id=1, source_target_pairs={{0,2},{2,0},{1,3},{3,1},{4,6},{6,4},{5,7},{7,5},{8,10},{10,8},{9,1... | collective-permute-start | bytes 98312 | tf_op jit(solution)/shard_map/ppermute | solution.py:414
  92.9 1.6 %collective-permute-done.6 = f32[8,2,4,128]{3,2,1,0:T(4,128)S(1)} collective-permute-done((f32[8,2,4,128]{3,2,1,0:T(4,128)S(1)}, f32[8,2,4,128]{3,2,1,0:T(4,128)S(1)}, u32[]{:S(2)}, u32[]{:S(2)}) %collective-permute-start.6) | collective-permute-done | bytes 32800 | tf_op jit(solution)/shard_map/ppermute | solution.py:414
  94.7 1.3 shard_map.101
  96.0 2.7 %collective-permute-start.7 = (f32[8,2,4,128]{3,2,1,0:T(4,128)S(1)}, f32[8,2,4,128]{3,2,1,0:T(4,128)S(1)}, u32[]{:S(2)}, u32[]{:S(2)}) collective-permute-start(f32[8,2,4,128]{3,2,1,0:T(4,128)S(1)} %pad_maximum_fusion.4), channel_id=1, source_target_pairs={{0,2},{2,0},{1,3},{3,1},{4,6},{6,4},{5,7},{7,5},{8,10},{10,8},{9,1... | collective-permute-start | bytes 98312 | tf_op jit(solution)/shard_map/ppermute | solution.py:423
  98.8 4.2 %collective-permute-start.8 = (f32[2,4,2,4,128]{4,3,2,1,0:T(4,128)S(1)}, f32[2,4,2,4,128]{4,3,2,1,0:T(4,128)S(1)}, u32[]{:S(2)}, u32[]{:S(2)}) collective-permute-start(f32[2,4,2,4,128]{4,3,2,1,0:T(4,128)S(1)} %pad_maximum_fusion.1), channel_id=1, source_target_pairs={{0,1},{1,0},{2,3},{3,2},{4,5},{5,4},{6,7},{7,6},{8,9},{9,8},{10,11... | collective-permute-start | bytes 98312 | tf_op jit(solution)/shard_map/ppermute | solution.py:418
  104.3 4.6 %all-to-all-start.3 = ((bf16[64,16,128]{2,1,0:T(8,128)(2,1)}), bf16[64,16,128]{2,1,0:T(8,128)(2,1)S(1)}, u32[]{:S(2)}, u32[]{:S(2)}) async-start(bf16[64,16,128]{2,1,0:T(8,128)(2,1)} %copy.51), calls=%async_computation.3 | async-start | bytes 524288 | tf_op jit(solution)/shard_map/all_to_all | solution.py:427
  109.0 1.6 %shard_map.103.slope_half = bf16[2,32,128,128]{3,2,1,0:T(8,128)(2,1)S(1)} custom-call(bf16[2,32,128,128]{3,2,1,0:T(8,128)(2,1)} %copy-done.1), custom_call_target="tpu_custom_call" | custom-call | flops 1000000000 | bytes 1000000 | tf_op jit(solution)/shard_map/pallas_call | solution.py:343
  110.6 3.0 %shard_map.102 = f32[4,8,2,128,128]{4,3,2,1,0:T(8,128)} custom-call(f32[4,2,8,128]{3,2,1,0:T(8,128)S(1)} %get-tuple-element.33.modes, f32[4,2,8,128]{3,2,1,0:T(8,128)S(1)} %get-tuple-element.32.grads), custom_call_target="tpu_custom_call" | custom-call | flops 1000000000 | bytes 4000000 | tf_op jit(solution)/shard_map/pallas_call | solution.py:359
  113.6 6.4 %all-to-all-done.3 = bf16[64,16,128]{2,1,0:T(8,128)(2,1)S(1)} async-done(((bf16[64,16,128]{2,1,0:T(8,128)(2,1)}), bf16[64,16,128]{2,1,0:T(8,128)(2,1)S(1)}, u32[]{:S(2)}, u32[]{:S(2)}) %all-to-all-start.3) | async-done | bytes 262176 | tf_op jit(solution)/shard_map/all_to_all | solution.py:427
  120.0 3.6 %collective-permute-start.9 = (bf16[64,16,128]{2,1,0:T(8,128)(2,1)S(1)}, bf16[64,16,128]{2,1,0:T(8,128)(2,1)S(1)}, u32[]{:S(2)}, u32[]{:S(2)}) collective-permute-start(bf16[64,16,128]{2,1,0:T(8,128)(2,1)S(1)} %all-to-all-done.3), channel_id=1, source_target_pairs={{0,1},{1,0},{2,3},{3,2},{4,5},{5,4},{6,7},{7,6},{8,9},{9,8},{10,11... | collective-permute-start | bytes 786440 | tf_op jit(solution)/shard_map/ppermute | solution.py:429
  124.8 3.0 %shard_map.105 = bf16[2,32,128,128]{3,2,1,0:T(8,128)(2,1)} custom-call(s32[2]{0:T(128)S(1)} %pad_add_fusion.place, f32[2,32,8,256]{3,2,1,0:T(8,128)S(1)} %shard_map.104.own_rows, bf16[32,2,16,128]{3,2,1,0:T(8,128)(2,1)S(1)} %bitcast.75, bf16[2,32,128,128]{3,2,1,0:T(8,128)(2,1)S(1)} %shard_map.103.slope_half, bf16[128,128]{1,0:T(8,128)(2,1)S(1)} %copy-done.10, ...), custom_call_target="tpu_custom_call" | custom-call | flops 2000000000 | bytes 1000000 | tf_op jit(solution)/shard_map/pallas_call | solution.py:343
  (77 shorter events, 11.3 us)
Async XLA Ops:
  3.9 5.7 %copy-start.4 = (bf16[1024,256]{1,0:T(8,128)(2,1)}, bf16[1024,256]{1,0:T(8,128)(2,1)S(1)}, u32[]{:S(2)}) copy-start(bf16[1024,256]{1,0:T(8,128)(2,1)S(1)} %get-tuple-element.17.y_table) | copy-start | bytes 1572868
  3.9 4.9 %collective-permute-start = (f32[32,2,16,128]{3,2,1,0:T(8,128)S(1)}, f32[32,2,16,128]{3,2,1,0:T(8,128)S(1)}, u32[]{:S(2)}, u32[]{:S(2)}) collective-permute-start(f32[32,2,16,128]{3,2,1,0:T(8,128)S(1)} %get-tuple-element.18), channel_id=1, source_target_pairs={{0,1},{1,0},{2,3},{3,2},{4,5},{5,4},{6,7},{7,6},{8,9},{9,8},{10,11... | collective-permute-start | bytes 1572872 | tf_op jit(solution)/shard_map/ppermute | solution.py:408
  7.2 13.3 %copy-start.2 = (bf16[4,8,2,128,128]{4,3,2,1,0:T(8,128)(2,1)S(1)}, bf16[4,8,2,128,128]{4,3,2,1,0:T(8,128)(2,1)}, u32[]{:S(2)}) copy-start(bf16[4,8,2,128,128]{4,3,2,1,0:T(8,128)(2,1)} %param.10) | copy-start | bytes 6291460
  8.2 24.2 %copy-start.13 = (f32[16,2,64,2,2,1]{2,0,4,3,5,1:T(8,128)S(1)}, f32[16,2,64,2,2,1]{2,0,4,3,5,1:T(8,128)}, u32[]{:S(2)}) copy-start(f32[16,2,64,2,2,1]{2,0,4,3,5,1:T(8,128)} %constant.84) | copy-start | bytes 98308
  9.6 22.8 %all-to-all-start = ((bf16[64,16,128]{2,1,0:T(8,128)(2,1)}), bf16[64,16,128]{2,1,0:T(8,128)(2,1)S(1)}, u32[]{:S(2)}, u32[]{:S(2)}) async-start(bf16[64,16,128]{2,1,0:T(8,128)(2,1)} %bitcast.5), calls=%async_computation | async-start | bytes 524288 | tf_op jit(solution)/shard_map/all_to_all | solution.py:410
  21.6 15.5 %collective-permute-start.2 = (bf16[4,4,2,128,128]{4,3,2,1,0:T(8,128)(2,1)}, bf16[4,4,2,128,128]{4,3,2,1,0:T(8,128)(2,1)S(1)}, u32[]{:S(2)}, u32[]{:S(2)}) collective-permute-start(bf16[4,4,2,128,128]{4,3,2,1,0:T(8,128)(2,1)} %dynamic-slice_bitcast_fusion), channel_id=1, source_target_pairs={{0,1},{1,0},{2,3},{3,2},{4,5},{5,4},{6,7},{7,6},{8,9},{9,8},{10,11... | collective-permute-start | bytes 3145736 | tf_op jit(solution)/shard_map/ppermute | solution.py:398
  32.7 4.4 %collective-permute-start.1 = (f32[8,2,4,128]{3,2,1,0:T(4,128)S(1)}, f32[8,2,4,128]{3,2,1,0:T(4,128)S(1)}, u32[]{:S(2)}, u32[]{:S(2)}) collective-permute-start(f32[8,2,4,128]{3,2,1,0:T(4,128)S(1)} %copy_select_fusion.1), channel_id=1, source_target_pairs={{0,2},{2,0},{1,3},{3,1},{4,6},{6,4},{5,7},{7,5},{8,10},{10,8},{9,1... | collective-permute-start | bytes 98312 | tf_op jit(solution)/shard_map/ppermute | solution.py:414
  38.1 27.0 %copy-start.5 = (bf16[1024,256]{1,0:T(8,128)(2,1)S(1)}, bf16[1024,256]{1,0:T(8,128)(2,1)}, u32[]{:S(2)}) copy-start(bf16[1024,256]{1,0:T(8,128)(2,1)} %copy-done.4) | copy-start | bytes 1572868
  38.2 4.4 %collective-permute-start.3 = (f32[8,2,4,128]{3,2,1,0:T(4,128)S(1)}, f32[8,2,4,128]{3,2,1,0:T(4,128)S(1)}, u32[]{:S(2)}, u32[]{:S(2)}) collective-permute-start(f32[8,2,4,128]{3,2,1,0:T(4,128)S(1)} %pad_maximum_fusion.3), channel_id=1, source_target_pairs={{0,2},{2,0},{1,3},{3,1},{4,6},{6,4},{5,7},{7,5},{8,10},{10,8},{9,1... | collective-permute-start | bytes 98312 | tf_op jit(solution)/shard_map/ppermute | solution.py:423
  43.1 23.1 %copy-start.8 = (bf16[384,256]{1,0:T(8,128)(2,1)S(1)}, bf16[384,256]{1,0:T(8,128)(2,1)}, u32[]{:S(2)}) copy-start(bf16[384,256]{1,0:T(8,128)(2,1)} %copy-done.7) | copy-start | bytes 589828
  43.2 22.9 %copy-start = (bf16[2,32,128,128]{3,2,1,0:T(8,128)(2,1)S(1)}, bf16[2,32,128,128]{3,2,1,0:T(8,128)(2,1)}, u32[]{:S(2)}) copy-start(bf16[2,32,128,128]{3,2,1,0:T(8,128)(2,1)} %field.3) | copy-start | bytes 6291460
  43.3 22.9 %copy-start.3 = (bf16[2,32,128,128]{3,2,1,0:T(8,128)(2,1)S(1)}, bf16[2,32,128,128]{3,2,1,0:T(8,128)(2,1)}, u32[]{:S(2)}) copy-start(bf16[2,32,128,128]{3,2,1,0:T(8,128)(2,1)} %cotangent.1) | copy-start | bytes 6291460
  43.3 22.9 %copy-start.10 = (bf16[128,128]{1,0:T(8,128)(2,1)S(1)}, bf16[128,128]{1,0:T(8,128)(2,1)}, u32[]{:S(2)}) copy-start(bf16[128,128]{1,0:T(8,128)(2,1)} %pointwise.3) | copy-start | bytes 98308
  43.3 22.9 %copy-start.11 = (f32[128]{0:T(128)S(1)}, f32[128]{0:T(128)}, u32[]{:S(2)}) copy-start(f32[128]{0:T(128)} %param.12) | copy-start | bytes 1540
  60.0 6.2 %collective-permute-start.4 = (bf16[64,16,128]{2,1,0:T(8,128)(2,1)S(1)}, bf16[64,16,128]{2,1,0:T(8,128)(2,1)S(1)}, u32[]{:S(2)}, u32[]{:S(2)}) collective-permute-start(bf16[64,16,128]{2,1,0:T(8,128)(2,1)S(1)} %all_to_all.20), channel_id=1, source_target_pairs={{0,1},{1,0},{2,3},{3,2},{4,5},{5,4},{6,7},{7,6},{8,9},{9,8},{10,11... | collective-permute-start | bytes 786440 | tf_op jit(solution)/shard_map/ppermute | solution.py:429
  71.7 2.0 %collective-permute-start.5 = (f32[32,2,16,128]{3,2,1,0:T(8,128)S(1)}, f32[32,2,16,128]{3,2,1,0:T(8,128)S(1)}, u32[]{:S(2)}, u32[]{:S(2)}) collective-permute-start(f32[32,2,16,128]{3,2,1,0:T(8,128)S(1)} %get-tuple-element.23), channel_id=1, source_target_pairs={{0,1},{1,0},{2,3},{3,2},{4,5},{5,4},{6,7},{7,6},{8,9},{9,8},{10,11... | collective-permute-start | bytes 1572872 | tf_op jit(solution)/shard_map/ppermute | solution.py:408
  73.3 22.7 %copy-start.1 = (bf16[2,32,128,128]{3,2,1,0:T(8,128)(2,1)}, bf16[2,32,128,128]{3,2,1,0:T(8,128)(2,1)S(1)}, u32[]{:S(2)}) copy-start(bf16[2,32,128,128]{3,2,1,0:T(8,128)(2,1)S(1)} %get-tuple-element.26.source) | copy-start | bytes 6291460
  90.2 4.4 %collective-permute-start.6 = (f32[8,2,4,128]{3,2,1,0:T(4,128)S(1)}, f32[8,2,4,128]{3,2,1,0:T(4,128)S(1)}, u32[]{:S(2)}, u32[]{:S(2)}) collective-permute-start(f32[8,2,4,128]{3,2,1,0:T(4,128)S(1)} %copy_select_fusion), channel_id=1, source_target_pairs={{0,2},{2,0},{1,3},{3,1},{4,6},{6,4},{5,7},{7,5},{8,10},{10,8},{9,1... | collective-permute-start | bytes 98312 | tf_op jit(solution)/shard_map/ppermute | solution.py:414
  96.0 7.0 %collective-permute-start.7 = (f32[8,2,4,128]{3,2,1,0:T(4,128)S(1)}, f32[8,2,4,128]{3,2,1,0:T(4,128)S(1)}, u32[]{:S(2)}, u32[]{:S(2)}) collective-permute-start(f32[8,2,4,128]{3,2,1,0:T(4,128)S(1)} %pad_maximum_fusion.4), channel_id=1, source_target_pairs={{0,2},{2,0},{1,3},{3,1},{4,6},{6,4},{5,7},{7,5},{8,10},{10,8},{9,1... | collective-permute-start | bytes 98312 | tf_op jit(solution)/shard_map/ppermute | solution.py:423
  98.8 11.7 %collective-permute-start.8 = (f32[2,4,2,4,128]{4,3,2,1,0:T(4,128)S(1)}, f32[2,4,2,4,128]{4,3,2,1,0:T(4,128)S(1)}, u32[]{:S(2)}, u32[]{:S(2)}) collective-permute-start(f32[2,4,2,4,128]{4,3,2,1,0:T(4,128)S(1)} %pad_maximum_fusion.1), channel_id=1, source_target_pairs={{0,1},{1,0},{2,3},{3,2},{4,5},{5,4},{6,7},{7,6},{8,9},{9,8},{10,11... | collective-permute-start | bytes 98312 | tf_op jit(solution)/shard_map/ppermute | solution.py:418
  104.3 15.6 %all-to-all-start.3 = ((bf16[64,16,128]{2,1,0:T(8,128)(2,1)}), bf16[64,16,128]{2,1,0:T(8,128)(2,1)S(1)}, u32[]{:S(2)}, u32[]{:S(2)}) async-start(bf16[64,16,128]{2,1,0:T(8,128)(2,1)} %copy.51), calls=%async_computation.3 | async-start | bytes 524288 | tf_op jit(solution)/shard_map/all_to_all | solution.py:427
  110.6 13.0 %copy-start.6 = (bf16[1024,256]{1,0:T(8,128)(2,1)S(1)}, bf16[1024,256]{1,0:T(8,128)(2,1)}, u32[]{:S(2)}) copy-start(bf16[1024,256]{1,0:T(8,128)(2,1)} %copy-done.4) | copy-start | bytes 1572868
  113.6 11.2 %copy-start.9 = (bf16[384,256]{1,0:T(8,128)(2,1)S(1)}, bf16[384,256]{1,0:T(8,128)(2,1)}, u32[]{:S(2)}) copy-start(bf16[384,256]{1,0:T(8,128)(2,1)} %copy-done.7) | copy-start | bytes 589828
  120.0 4.8 %collective-permute-start.9 = (bf16[64,16,128]{2,1,0:T(8,128)(2,1)S(1)}, bf16[64,16,128]{2,1,0:T(8,128)(2,1)S(1)}, u32[]{:S(2)}, u32[]{:S(2)}) collective-permute-start(bf16[64,16,128]{2,1,0:T(8,128)(2,1)S(1)} %all-to-all-done.3), channel_id=1, source_target_pairs={{0,1},{1,0},{2,3},{3,2},{4,5},{5,4},{6,7},{7,6},{8,9},{9,8},{10,11... | collective-permute-start | bytes 786440 | tf_op jit(solution)/shard_map/ppermute | solution.py:429
  (2 other events, 11.1 us)

commit v2 on v1

--- a/solution.py
+++ b/solution.py
@@ -135,8 +135,8 @@
         high, low = split(block.reshape(block.shape[0] * 8, block.shape[2]))
         planes = folded(y_table[:2 * count], high) + matmul(y_table[:count], low)
         planes = planes.reshape(2 * MY, 8, 2 * channels)
-        target[:, half, 0:8, :] = planes[:, :, :channels]
-        target[:, half, 8:16, :] = planes[:, :, channels:]
+        planes = jnp.concatenate([planes[:, :, :channels], planes[:, :, channels:]], axis=1)
+        target[:, half] = planes.astype(target.dtype)
 
 
 def y_inverse(source, half, y_table):
@@ -398,6 +398,7 @@
     other_weights = lax.ppermute(send, "fsdp", CORE_SWAP)
 
     message = jax.ShapeDtypeStruct((2 * MY, 2, 8 * x_rows, channels), f32)
+    sent = jax.ShapeDtypeStruct(message.shape, bf16)
     lifted_form = pltpu.VMEM((y_rows, 2 * MZ, 2 * channels), f32)
     own_form = pltpu.VMEM((2, y_rows, 8, 2 * channels), f32)
 
@@ -405,7 +406,7 @@
         return value * weight[None, None, :, None]
 
     def to_modes(send, keep):
-        planes = keep + lax.ppermute(send, "fsdp", CORE_SWAP)
+        planes = keep + lax.ppermute(send, "fsdp", CORE_SWAP).astype(f32)
         planes = planes.astype(bf16).reshape(slabs, x_rows * 8, channels)
         whole_x = lax.all_to_all(planes, "slab", split_axis=0, concat_axis=0, tiled=True)
         whole_x = whole_x.reshape(slabs, x_rows, 2, 4, channels).astype(f32)
@@ -441,7 +442,7 @@
     )
     send, lifted, z_table, y_table = device_call(
         lift_kernel, (place, fields, z_all, y_all), (smem, hbm, hbm, hbm),
-        (message, lifted_form) + forms, (vmem,) * 4,
+        (sent, lifted_form) + forms, (vmem,) * 4,
         [cells, sems, pltpu.SemaphoreType.DMA((2,))], 10**9,
     )
     keep, = device_call(
@@ -460,7 +461,7 @@
         slope_kernel,
         (place, own_rows, other, fields, cotangent, pointwise, bias, z_table, y_table),
         (smem,) + (vmem,) * 8,
-        (vmem(fields.shape, bf16), message, lifted_form), (vmem,) * 3,
+        (vmem(fields.shape, bf16), sent, lifted_form), (vmem,) * 3,
         [lifted_form], 4 * 10**9,
     )
     keep, slope_half = device_call(

time: 128 us -> 128 us (level)
  transfers between devices with their start and end apart: 12 -> 12, of which waited for: 9 -> 8; matrix products, arithmetic and copies ran while one was open for 2% -> 2% of each run, Pallas kernels for 6% -> 6%
where the time goes in v2:
time: 128 us; the launch traced here: 127 us
  starting transfers between devices  43.7 us (34%)
  blocking collectives  32.8 us (26%)
  waiting for transfers between devices  23.5 us (18%)
  Pallas kernels  21.1 us (16%)
  local copies, waits for them, and re-layouts  2.25 us (2%)
  other arithmetic  1.42 us (1%)
  matrix products  1.29 us (1%)
    pallas_call x10, Pallas kernels, device_call(): pl.pallas_call(kernel, in_specs=[pl.BlockSpec(memory_space=space) for spa...  18.1 us
    all_to_all x1, blocking collectives, to_planes(): lax.all_to_all(planes, 'slab', split_axis=0, concat_axis=0, tiled=True)  16.7 us
    all_to_all x1, blocking collectives, to_modes(): lax.all_to_all(planes, 'slab', split_axis=0, concat_axis=0, tiled=True)  16.1 us
    all_to_all x1, starting transfers between devices, to_modes(): lax.all_to_all(planes, 'slab', split_axis=0, concat_axis=0, tiled=True)  10.9 us
    all_to_all x1, waiting for transfers between devices, to_modes(): lax.all_to_all(planes, 'slab', split_axis=0, concat_axis=0, tiled=True)  10.2 us
    ppermute x2, starting transfers between devices, to_planes(): other = lax.ppermute(planes, 'fsdp', CORE_SWAP)  8.67 us
    all_to_all x1, waiting for transfers between devices, to_planes(): lax.all_to_all(planes, 'slab', split_axis=0, concat_axis=0, tiled=True)  6.39 us
    ppermute x2, starting transfers between devices, to_modes(): modes = keep + lax.ppermute(send, 'fsdp', CHIP_SWAP)  5.42 us
  transfers between devices with their start and end apart: 12, of which 8 were waited for; matrix products, arithmetic and copies ran while one was open for 2% of the time, Pallas kernels for 6%

profile of v2, /device:TPU:1, one launch (start us, length us, event | category | flops | bytes accessed | tf_op | source)
XLA Modules:
  0.0 127.2 jit_solution(8183452592951902941)
XLA Ops:
  0.7 3.2 %shard_map.95 = (bf16[32,2,16,128]{3,2,1,0:T(8,128)(2,1)S(1)}, f32[32,32,256]{2,1,0:T(8,128)S(1)}, bf16[384,256]{1,0:T(8,128)(2,1)S(1)}, bf16[1024,256]{1,0:T(8,128)(2,1)S(1)}) custom-call(s32[2]{0:T(128)S(1)} %pad_add_fusion.place, bf16[2,32,128,128]{3,2,1,0:T(8,128)(2,1)} %field.3, bf16[384,256]{1,0:T(8,128)(2,1)} %constant.79.clone.z_tables, ...), custom_call_target="tpu_custom_call" | custom-call | flops 1000000000 | bytes 1000000 | tf_op jit(solution)/shard_map/pallas_call | solution.py:343
  3.9 3.3 %collective-permute-start = (bf16[32,2,16,128]{3,2,1,0:T(8,128)(2,1)S(1)}, bf16[32,2,16,128]{3,2,1,0:T(8,128)(2,1)S(1)}, u32[]{:S(2)}, u32[]{:S(2)}) collective-permute-start(bf16[32,2,16,128]{3,2,1,0:T(8,128)(2,1)S(1)} %get-tuple-element.18), channel_id=1, source_target_pairs={{0,1},{1,0},{2,3},{3,2},{4,5},{5,4},{6,7},{7,6},{8,9},{9,8},{10,11... | collective-permute-start | bytes 786440 | tf_op jit(solution)/shard_map/ppermute | solution.py:409
  9.2 10.9 %all-to-all-start = ((bf16[64,16,128]{2,1,0:T(8,128)(2,1)}), bf16[64,16,128]{2,1,0:T(8,128)(2,1)S(1)}, u32[]{:S(2)}, u32[]{:S(2)}) async-start(bf16[64,16,128]{2,1,0:T(8,128)(2,1)} %bitcast.5), calls=%async_computation | async-start | bytes 524288 | tf_op jit(solution)/shard_map/all_to_all | solution.py:411
  21.8 10.2 %all-to-all-done = bf16[64,16,128]{2,1,0:T(8,128)(2,1)S(1)} async-done(((bf16[64,16,128]{2,1,0:T(8,128)(2,1)}), bf16[64,16,128]{2,1,0:T(8,128)(2,1)S(1)}, u32[]{:S(2)}, u32[]{:S(2)}) %all-to-all-start) | async-done | bytes 262176 | tf_op jit(solution)/shard_map/all_to_all | solution.py:411
  32.3 2.7 %collective-permute-start.1 = (f32[8,2,4,128]{3,2,1,0:T(4,128)S(1)}, f32[8,2,4,128]{3,2,1,0:T(4,128)S(1)}, u32[]{:S(2)}, u32[]{:S(2)}) collective-permute-start(f32[8,2,4,128]{3,2,1,0:T(4,128)S(1)} %copy_select_fusion.1), channel_id=1, source_target_pairs={{0,2},{2,0},{1,3},{3,1},{4,6},{6,4},{5,7},{7,5},{8,10},{10,8},{9,1... | collective-permute-start | bytes 98312 | tf_op jit(solution)/shard_map/ppermute | solution.py:415
  35.0 1.6 %collective-permute-done.1 = f32[8,2,4,128]{3,2,1,0:T(4,128)S(1)} collective-permute-done((f32[8,2,4,128]{3,2,1,0:T(4,128)S(1)}, f32[8,2,4,128]{3,2,1,0:T(4,128)S(1)}, u32[]{:S(2)}, u32[]{:S(2)}) %collective-permute-start.1) | collective-permute-done | bytes 32800 | tf_op jit(solution)/shard_map/ppermute | solution.py:415
  37.8 2.7 %collective-permute-start.3 = (f32[8,2,4,128]{3,2,1,0:T(4,128)S(1)}, f32[8,2,4,128]{3,2,1,0:T(4,128)S(1)}, u32[]{:S(2)}, u32[]{:S(2)}) collective-permute-start(f32[8,2,4,128]{3,2,1,0:T(4,128)S(1)} %pad_maximum_fusion.3), channel_id=1, source_target_pairs={{0,2},{2,0},{1,3},{3,1},{4,6},{6,4},{5,7},{7,5},{8,10},{10,8},{9,1... | collective-permute-start | bytes 98312 | tf_op jit(solution)/shard_map/ppermute | solution.py:424
  40.5 1.6 %collective-permute-done.3 = f32[8,2,4,128]{3,2,1,0:T(4,128)S(1)} collective-permute-done((f32[8,2,4,128]{3,2,1,0:T(4,128)S(1)}, f32[8,2,4,128]{3,2,1,0:T(4,128)S(1)}, u32[]{:S(2)}, u32[]{:S(2)}) %collective-permute-start.3) | collective-permute-done | bytes 32800 | tf_op jit(solution)/shard_map/ppermute | solution.py:424
  42.9 16.7 %all_to_all.20 = bf16[64,16,128]{2,1,0:T(8,128)(2,1)S(1)} all-to-all(bf16[64,16,128]{2,1,0:T(8,128)(2,1)S(1)} %copy.43), channel_id=1, replica_groups=mesh['slab'=64,'fsdp'=4] {'slab'}, dimensions={0} | all-to-all | bytes 524288 | tf_op jit(solution)/shard_map/all_to_all | solution.py:428
  59.6 5.0 %collective-permute-start.4 = (bf16[64,16,128]{2,1,0:T(8,128)(2,1)S(1)}, bf16[64,16,128]{2,1,0:T(8,128)(2,1)S(1)}, u32[]{:S(2)}, u32[]{:S(2)}) collective-permute-start(bf16[64,16,128]{2,1,0:T(8,128)(2,1)S(1)} %all_to_all.20), channel_id=1, source_target_pairs={{0,1},{1,0},{2,3},{3,2},{4,5},{5,4},{6,7},{7,6},{8,9},{9,8},{10,11... | collective-permute-start | bytes 786440 | tf_op jit(solution)/shard_map/ppermute | solution.py:430
  65.8 5.5 %shard_map.99 = (bf16[2,32,128,128]{3,2,1,0:T(8,128)(2,1)S(1)}, bf16[32,2,16,128]{3,2,1,0:T(8,128)(2,1)S(1)}, f32[32,32,256]{2,1,0:T(8,128)S(1)}) custom-call(s32[2]{0:T(128)S(1)} %pad_add_fusion.place, f32[2,32,8,256]{3,2,1,0:T(8,128)S(1)} %shard_map.98.own_rows, bf16[32,2,16,128]{3,2,1,0:T(8,128)(2,1)S(1)} %bitcast.74, ...), custom_call_target="tpu_custom_call" | custom-call | flops 4000000000 | bytes 1000000 | tf_op jit(solution)/shard_map/pallas_call | solution.py:343
  71.8 1.1 shard_map.100
  73.0 16.1 %all_to_all.21 = bf16[64,16,128]{2,1,0:T(8,128)(2,1)S(1)} all-to-all(bf16[64,16,128]{2,1,0:T(8,128)(2,1)S(1)} %bitcast.81), channel_id=1, replica_groups=mesh['slab'=64,'fsdp'=4] {'slab'}, dimensions={0} | all-to-all | bytes 524288 | tf_op jit(solution)/shard_map/all_to_all | solution.py:411
  89.4 2.7 %collective-permute-start.6 = (f32[8,2,4,128]{3,2,1,0:T(4,128)S(1)}, f32[8,2,4,128]{3,2,1,0:T(4,128)S(1)}, u32[]{:S(2)}, u32[]{:S(2)}) collective-permute-start(f32[8,2,4,128]{3,2,1,0:T(4,128)S(1)} %copy_select_fusion), channel_id=1, source_target_pairs={{0,2},{2,0},{1,3},{3,1},{4,6},{6,4},{5,7},{7,5},{8,10},{10,8},{9,1... | collective-permute-start | bytes 98312 | tf_op jit(solution)/shard_map/ppermute | solution.py:415
  92.1 1.6 %collective-permute-done.6 = f32[8,2,4,128]{3,2,1,0:T(4,128)S(1)} collective-permute-done((f32[8,2,4,128]{3,2,1,0:T(4,128)S(1)}, f32[8,2,4,128]{3,2,1,0:T(4,128)S(1)}, u32[]{:S(2)}, u32[]{:S(2)}) %collective-permute-start.6) | collective-permute-done | bytes 32800 | tf_op jit(solution)/shard_map/ppermute | solution.py:415
  93.9 1.3 %shard_map.101 = f32[4,2,8,128]{3,2,1,0:T(8,128)S(1)} custom-call(s32[2]{0:T(128)S(1)} %pad_add_fusion.place, f32[4,2,8,128]{3,2,1,0:T(8,128)S(1)} %maximum_multiply_fusion.grads, bf16[4,2,4,2,128,128]{5,4,3,2,1,0:T(8,128)(2,1)S(1)} %bitcast.71, bf16[4,4,2,128,128]{4,3,2,1,0:T(8,128)(2,1)S(1)} %collective-permute-done.2.other), custom_call_target="tpu_custom_call" | custom-call | flops 1000000000 | bytes 1000000 | tf_op jit(solution)/shard_map/pallas_call | solution.py:343
  95.2 2.7 %collective-permute-start.7 = (f32[8,2,4,128]{3,2,1,0:T(4,128)S(1)}, f32[8,2,4,128]{3,2,1,0:T(4,128)S(1)}, u32[]{:S(2)}, u32[]{:S(2)}) collective-permute-start(f32[8,2,4,128]{3,2,1,0:T(4,128)S(1)} %pad_maximum_fusion.4), channel_id=1, source_target_pairs={{0,2},{2,0},{1,3},{3,1},{4,6},{6,4},{5,7},{7,5},{8,10},{10,8},{9,1... | collective-permute-start | bytes 98312 | tf_op jit(solution)/shard_map/ppermute | solution.py:424
  98.0 4.2 %collective-permute-start.8 = (f32[2,4,2,4,128]{4,3,2,1,0:T(4,128)S(1)}, f32[2,4,2,4,128]{4,3,2,1,0:T(4,128)S(1)}, u32[]{:S(2)}, u32[]{:S(2)}) collective-permute-start(f32[2,4,2,4,128]{4,3,2,1,0:T(4,128)S(1)} %pad_maximum_fusion.1), channel_id=1, source_target_pairs={{0,1},{1,0},{2,3},{3,2},{4,5},{5,4},{6,7},{7,6},{8,9},{9,8},{10,11... | collective-permute-start | bytes 98312 | tf_op jit(solution)/shard_map/ppermute | solution.py:419
  103.6 4.6 %all-to-all-start.3 = ((bf16[64,16,128]{2,1,0:T(8,128)(2,1)}), bf16[64,16,128]{2,1,0:T(8,128)(2,1)S(1)}, u32[]{:S(2)}, u32[]{:S(2)}) async-start(bf16[64,16,128]{2,1,0:T(8,128)(2,1)} %copy.51), calls=%async_computation.3 | async-start | bytes 524288 | tf_op jit(solution)/shard_map/all_to_all | solution.py:428
  108.2 1.6 %shard_map.103.slope_half = bf16[2,32,128,128]{3,2,1,0:T(8,128)(2,1)S(1)} custom-call(bf16[2,32,128,128]{3,2,1,0:T(8,128)(2,1)} %copy-done.1), custom_call_target="tpu_custom_call" | custom-call | flops 1000000000 | bytes 1000000 | tf_op jit(solution)/shard_map/pallas_call | solution.py:343
  109.8 3.0 %shard_map.102 = f32[4,8,2,128,128]{4,3,2,1,0:T(8,128)} custom-call(f32[4,2,8,128]{3,2,1,0:T(8,128)S(1)} %get-tuple-element.33.modes, f32[4,2,8,128]{3,2,1,0:T(8,128)S(1)} %get-tuple-element.32.grads), custom_call_target="tpu_custom_call" | custom-call | flops 1000000000 | bytes 4000000 | tf_op jit(solution)/shard_map/pallas_call | solution.py:359
  112.8 6.4 %all-to-all-done.3 = bf16[64,16,128]{2,1,0:T(8,128)(2,1)S(1)} async-done(((bf16[64,16,128]{2,1,0:T(8,128)(2,1)}), bf16[64,16,128]{2,1,0:T(8,128)(2,1)S(1)}, u32[]{:S(2)}, u32[]{:S(2)}) %all-to-all-start.3) | async-done | bytes 262176 | tf_op jit(solution)/shard_map/all_to_all | solution.py:428
  119.2 3.6 %collective-permute-start.9 = (bf16[64,16,128]{2,1,0:T(8,128)(2,1)S(1)}, bf16[64,16,128]{2,1,0:T(8,128)(2,1)S(1)}, u32[]{:S(2)}, u32[]{:S(2)}) collective-permute-start(bf16[64,16,128]{2,1,0:T(8,128)(2,1)S(1)} %all-to-all-done.3), channel_id=1, source_target_pairs={{0,1},{1,0},{2,3},{3,2},{4,5},{5,4},{6,7},{7,6},{8,9},{9,8},{10,11... | collective-permute-start | bytes 786440 | tf_op jit(solution)/shard_map/ppermute | solution.py:430
  124.0 3.0 %shard_map.105 = bf16[2,32,128,128]{3,2,1,0:T(8,128)(2,1)} custom-call(s32[2]{0:T(128)S(1)} %pad_add_fusion.place, f32[2,32,8,256]{3,2,1,0:T(8,128)S(1)} %shard_map.104.own_rows, bf16[32,2,16,128]{3,2,1,0:T(8,128)(2,1)S(1)} %bitcast.75, bf16[2,32,128,128]{3,2,1,0:T(8,128)(2,1)S(1)} %shard_map.103.slope_half, bf16[128,128]{1,0:T(8,128)(2,1)S(1)} %copy-done.10, ...), custom_call_target="tpu_custom_call" | custom-call | flops 2000000000 | bytes 1000000 | tf_op jit(solution)/shard_map/pallas_call | solution.py:343
  (77 shorter events, 10.5 us)
Async XLA Ops:
  3.9 4.5 %collective-permute-start = (bf16[32,2,16,128]{3,2,1,0:T(8,128)(2,1)S(1)}, bf16[32,2,16,128]{3,2,1,0:T(8,128)(2,1)S(1)}, u32[]{:S(2)}, u32[]{:S(2)}) collective-permute-start(bf16[32,2,16,128]{3,2,1,0:T(8,128)(2,1)S(1)} %get-tuple-element.18), channel_id=1, source_target_pairs={{0,1},{1,0},{2,3},{3,2},{4,5},{5,4},{6,7},{7,6},{8,9},{9,8},{10,11... | collective-permute-start | bytes 786440 | tf_op jit(solution)/shard_map/ppermute | solution.py:409
  7.2 12.9 %copy-start.2 = (bf16[4,8,2,128,128]{4,3,2,1,0:T(8,128)(2,1)S(1)}, bf16[4,8,2,128,128]{4,3,2,1,0:T(8,128)(2,1)}, u32[]{:S(2)}) copy-start(bf16[4,8,2,128,128]{4,3,2,1,0:T(8,128)(2,1)} %param.10) | copy-start | bytes 6291460
  8.2 23.8 %copy-start.13 = (f32[16,2,64,2,2,1]{2,0,4,3,5,1:T(8,128)S(1)}, f32[16,2,64,2,2,1]{2,0,4,3,5,1:T(8,128)}, u32[]{:S(2)}) copy-start(f32[16,2,64,2,2,1]{2,0,4,3,5,1:T(8,128)} %constant.84) | copy-start | bytes 98308
  9.2 22.8 %all-to-all-start = ((bf16[64,16,128]{2,1,0:T(8,128)(2,1)}), bf16[64,16,128]{2,1,0:T(8,128)(2,1)S(1)}, u32[]{:S(2)}, u32[]{:S(2)}) async-start(bf16[64,16,128]{2,1,0:T(8,128)(2,1)} %bitcast.5), calls=%async_computation | async-start | bytes 524288 | tf_op jit(solution)/shard_map/all_to_all | solution.py:411
  21.2 15.5 %collective-permute-start.2 = (bf16[4,4,2,128,128]{4,3,2,1,0:T(8,128)(2,1)}, bf16[4,4,2,128,128]{4,3,2,1,0:T(8,128)(2,1)S(1)}, u32[]{:S(2)}, u32[]{:S(2)}) collective-permute-start(bf16[4,4,2,128,128]{4,3,2,1,0:T(8,128)(2,1)} %dynamic-slice_bitcast_fusion), channel_id=1, source_target_pairs={{0,1},{1,0},{2,3},{3,2},{4,5},{5,4},{6,7},{7,6},{8,9},{9,8},{10,11... | collective-permute-start | bytes 3145736 | tf_op jit(solution)/shard_map/ppermute | solution.py:398
  32.3 4.4 %collective-permute-start.1 = (f32[8,2,4,128]{3,2,1,0:T(4,128)S(1)}, f32[8,2,4,128]{3,2,1,0:T(4,128)S(1)}, u32[]{:S(2)}, u32[]{:S(2)}) collective-permute-start(f32[8,2,4,128]{3,2,1,0:T(4,128)S(1)} %copy_select_fusion.1), channel_id=1, source_target_pairs={{0,2},{2,0},{1,3},{3,1},{4,6},{6,4},{5,7},{7,5},{8,10},{10,8},{9,1... | collective-permute-start | bytes 98312 | tf_op jit(solution)/shard_map/ppermute | solution.py:415
  36.7 5.5 %copy-start.12 = (f32[16,2,64,2,2,1]{2,0,1,4,3,5:T(8,128)S(1)}, f32[16,2,64,2,2,1]{2,0,1,4,3,5:T(8,128)}, u32[]{:S(2)}) copy-start(f32[16,2,64,2,2,1]{2,0,1,4,3,5:T(8,128)} %constant.86) | copy-start | bytes 98308
  37.7 27.0 %copy-start.5 = (bf16[1024,256]{1,0:T(8,128)(2,1)S(1)}, bf16[1024,256]{1,0:T(8,128)(2,1)}, u32[]{:S(2)}) copy-start(bf16[1024,256]{1,0:T(8,128)(2,1)} %copy-done.4) | copy-start | bytes 1572868
  37.8 4.4 %collective-permute-start.3 = (f32[8,2,4,128]{3,2,1,0:T(4,128)S(1)}, f32[8,2,4,128]{3,2,1,0:T(4,128)S(1)}, u32[]{:S(2)}, u32[]{:S(2)}) collective-permute-start(f32[8,2,4,128]{3,2,1,0:T(4,128)S(1)} %pad_maximum_fusion.3), channel_id=1, source_target_pairs={{0,2},{2,0},{1,3},{3,1},{4,6},{6,4},{5,7},{7,5},{8,10},{10,8},{9,1... | collective-permute-start | bytes 98312 | tf_op jit(solution)/shard_map/ppermute | solution.py:424
  42.7 23.1 %copy-start.8 = (bf16[384,256]{1,0:T(8,128)(2,1)S(1)}, bf16[384,256]{1,0:T(8,128)(2,1)}, u32[]{:S(2)}) copy-start(bf16[384,256]{1,0:T(8,128)(2,1)} %copy-done.7) | copy-start | bytes 589828
  42.9 22.9 %copy-start = (bf16[2,32,128,128]{3,2,1,0:T(8,128)(2,1)S(1)}, bf16[2,32,128,128]{3,2,1,0:T(8,128)(2,1)}, u32[]{:S(2)}) copy-start(bf16[2,32,128,128]{3,2,1,0:T(8,128)(2,1)} %field.3) | copy-start | bytes 6291460
  42.9 22.9 %copy-start.3 = (bf16[2,32,128,128]{3,2,1,0:T(8,128)(2,1)S(1)}, bf16[2,32,128,128]{3,2,1,0:T(8,128)(2,1)}, u32[]{:S(2)}) copy-start(bf16[2,32,128,128]{3,2,1,0:T(8,128)(2,1)} %cotangent.1) | copy-start | bytes 6291460
  42.9 22.9 %copy-start.10 = (bf16[128,128]{1,0:T(8,128)(2,1)S(1)}, bf16[128,128]{1,0:T(8,128)(2,1)}, u32[]{:S(2)}) copy-start(bf16[128,128]{1,0:T(8,128)(2,1)} %pointwise.3) | copy-start | bytes 98308
  42.9 22.9 %copy-start.11 = (f32[128]{0:T(128)S(1)}, f32[128]{0:T(128)}, u32[]{:S(2)}) copy-start(f32[128]{0:T(128)} %param.12) | copy-start | bytes 1540
  59.6 6.2 %collective-permute-start.4 = (bf16[64,16,128]{2,1,0:T(8,128)(2,1)S(1)}, bf16[64,16,128]{2,1,0:T(8,128)(2,1)S(1)}, u32[]{:S(2)}, u32[]{:S(2)}) collective-permute-start(bf16[64,16,128]{2,1,0:T(8,128)(2,1)S(1)} %all_to_all.20), channel_id=1, source_target_pairs={{0,1},{1,0},{2,3},{3,2},{4,5},{5,4},{6,7},{7,6},{8,9},{9,8},{10,11... | collective-permute-start | bytes 786440 | tf_op jit(solution)/shard_map/ppermute | solution.py:430
  71.3 1.6 %collective-permute-start.5 = (bf16[32,2,16,128]{3,2,1,0:T(8,128)(2,1)S(1)}, bf16[32,2,16,128]{3,2,1,0:T(8,128)(2,1)S(1)}, u32[]{:S(2)}, u32[]{:S(2)}) collective-permute-start(bf16[32,2,16,128]{3,2,1,0:T(8,128)(2,1)S(1)} %get-tuple-element.23), channel_id=1, source_target_pairs={{0,1},{1,0},{2,3},{3,2},{4,5},{5,4},{6,7},{7,6},{8,9},{9,8},{10,11... | collective-permute-start | bytes 786440 | tf_op jit(solution)/shard_map/ppermute | solution.py:409
  72.9 22.3 %copy-start.1 = (bf16[2,32,128,128]{3,2,1,0:T(8,128)(2,1)}, bf16[2,32,128,128]{3,2,1,0:T(8,128)(2,1)S(1)}, u32[]{:S(2)}) copy-start(bf16[2,32,128,128]{3,2,1,0:T(8,128)(2,1)S(1)} %get-tuple-element.26.source) | copy-start | bytes 6291460
  89.4 4.4 %collective-permute-start.6 = (f32[8,2,4,128]{3,2,1,0:T(4,128)S(1)}, f32[8,2,4,128]{3,2,1,0:T(4,128)S(1)}, u32[]{:S(2)}, u32[]{:S(2)}) collective-permute-start(f32[8,2,4,128]{3,2,1,0:T(4,128)S(1)} %copy_select_fusion), channel_id=1, source_target_pairs={{0,2},{2,0},{1,3},{3,1},{4,6},{6,4},{5,7},{7,5},{8,10},{10,8},{9,1... | collective-permute-start | bytes 98312 | tf_op jit(solution)/shard_map/ppermute | solution.py:415
  95.2 7.0 %collective-permute-start.7 = (f32[8,2,4,128]{3,2,1,0:T(4,128)S(1)}, f32[8,2,4,128]{3,2,1,0:T(4,128)S(1)}, u32[]{:S(2)}, u32[]{:S(2)}) collective-permute-start(f32[8,2,4,128]{3,2,1,0:T(4,128)S(1)} %pad_maximum_fusion.4), channel_id=1, source_target_pairs={{0,2},{2,0},{1,3},{3,1},{4,6},{6,4},{5,7},{7,5},{8,10},{10,8},{9,1... | collective-permute-start | bytes 98312 | tf_op jit(solution)/shard_map/ppermute | solution.py:424
  98.0 11.7 %collective-permute-start.8 = (f32[2,4,2,4,128]{4,3,2,1,0:T(4,128)S(1)}, f32[2,4,2,4,128]{4,3,2,1,0:T(4,128)S(1)}, u32[]{:S(2)}, u32[]{:S(2)}) collective-permute-start(f32[2,4,2,4,128]{4,3,2,1,0:T(4,128)S(1)} %pad_maximum_fusion.1), channel_id=1, source_target_pairs={{0,1},{1,0},{2,3},{3,2},{4,5},{5,4},{6,7},{7,6},{8,9},{9,8},{10,11... | collective-permute-start | bytes 98312 | tf_op jit(solution)/shard_map/ppermute | solution.py:419
  103.6 15.6 %all-to-all-start.3 = ((bf16[64,16,128]{2,1,0:T(8,128)(2,1)}), bf16[64,16,128]{2,1,0:T(8,128)(2,1)S(1)}, u32[]{:S(2)}, u32[]{:S(2)}) async-start(bf16[64,16,128]{2,1,0:T(8,128)(2,1)} %copy.51), calls=%async_computation.3 | async-start | bytes 524288 | tf_op jit(solution)/shard_map/all_to_all | solution.py:428
  109.8 13.0 %copy-start.6 = (bf16[1024,256]{1,0:T(8,128)(2,1)S(1)}, bf16[1024,256]{1,0:T(8,128)(2,1)}, u32[]{:S(2)}) copy-start(bf16[1024,256]{1,0:T(8,128)(2,1)} %copy-done.4) | copy-start | bytes 1572868
  112.8 11.2 %copy-start.9 = (bf16[384,256]{1,0:T(8,128)(2,1)S(1)}, bf16[384,256]{1,0:T(8,128)(2,1)}, u32[]{:S(2)}) copy-start(bf16[384,256]{1,0:T(8,128)(2,1)} %copy-done.7) | copy-start | bytes 589828
  119.2 4.8 %collective-permute-start.9 = (bf16[64,16,128]{2,1,0:T(8,128)(2,1)S(1)}, bf16[64,16,128]{2,1,0:T(8,128)(2,1)S(1)}, u32[]{:S(2)}, u32[]{:S(2)}) collective-permute-start(bf16[64,16,128]{2,1,0:T(8,128)(2,1)S(1)} %all-to-all-done.3), channel_id=1, source_target_pairs={{0,1},{1,0},{2,3},{3,2},{4,5},{5,4},{6,7},{7,6},{8,9},{9,8},{10,11... | collective-permute-start | bytes 786440 | tf_op jit(solution)/shard_map/ppermute | solution.py:430
  (2 other events, 10.6 us)
